TPU v7x, 32 devices: a whole 2x2x4 slice. The times are simulated.
32 devices in a mesh: groups: 2 (over x), orb: 16 (over z, y, core).
Axes of the slice: x: 2, y: 2, z: 4, core: 2. Of those that a mesh axis runs over, the one named last changes fastest.
Arguments:
- phi: bfloat16 [512, 32768], P(('groups', 'orb')), parts along dimension 0, may hold values from -6 to 6
- offsets: int32 [512, 3], P('groups'), parts along dimension 0, may hold values from 0 to 1
- fetch: int32 [32, 16], P(('groups', 'orb')), parts along dimension 0, may hold values from -1 to 15, as said below
- task_pairs: int32 [1536, 2], P(('groups', 'orb')), parts along dimension 0, may hold values from 0 to 15, as said below
- task_count: int32 [32], P(('groups', 'orb')), parts along dimension 0, may hold values from 6 to 48, as said below
Outputs:
- exchange_potential: float32 [512, 32768], P(('groups', 'orb')), parts along dimension 0
There are 2 independent parts, one for each index of `groups`. A program takes and returns all parts, laid end to end along the dimension named above; each array names one. Nothing has to cross between parts.
Inputs may be any that keep to these rules, and one draw needn't show every extreme that they name: `fetch`: -1 means nothing is requested; device d requests 16 - 1 from itself, something from owner d + 1 (cyclic), and something from at least half of the owners. `task_pairs`: every owner named in a slot of a device has a request other than -1 in that device's fetch row; no owner is the first owner of more than 6 of one device's slots, and each device is the first owner of exactly 6 of its own slots. `task_count`: each count is 48 divided by 1, 2, 4 or 8.
All inputs are finite; a program needn't handle non-finite values.
Results may differ from a plain program's by a relative error of at most 0.0003.
Values may be sent and summed in bfloat16 or wider, within the bound.
No kernel may reach another device: no remote copies, remote signals or barrier semaphores. Data moves between devices by JAX's collectives and lax.ppermute only.
A program may use at most 128 MiB of HBM per device.

v0:
```python
import jax
import jax.numpy as jnp
from jax import lax
from jax.sharding import PartitionSpec as P

task_batch = 8


def sine_table(length):
    counter = jnp.arange(length).astype(jnp.float32) + 1.0
    return jnp.sqrt(2.0 / (length + 1)) * jnp.sin(
        jnp.pi * counter[:, None] * counter[None, :] / (length + 1)
    )


def inverse_eigen(length):
    counter = jnp.arange(length).astype(jnp.float32) + 1.0
    eigen = 2.0 - 2.0 * jnp.cos(jnp.pi * counter / (length + 1))
    total = eigen[:, None, None] + eigen[None, :, None] + eigen[None, None, :]
    return (1.0 / total).reshape(length, length * length)


def solve_box(density, table_x, table_yz, inverse):
    highest = lax.Precision.HIGHEST
    spectrum = jnp.einsum("kx,bxm->bkm", table_x, density, precision=highest)
    spectrum = jnp.einsum("bkm,nm->bkn", spectrum, table_yz, precision=highest)
    spectrum = spectrum * inverse[None]
    potential = jnp.einsum("kx,bxm->bkm", table_x, spectrum, precision=highest)
    return jnp.einsum("bkm,nm->bkn", potential, table_yz, precision=highest)


def move_flat(patch_flat, offset_diff, length):
    half_cells = length // 2
    volume = length * length * length
    margin = half_cells * (length * length + length + 1)
    places = jnp.arange(volume)
    coord_x = places // (length * length)
    coord_y = places // length % length
    coord_z = places % length
    step_x = coord_x + half_cells * offset_diff[0]
    step_y = coord_y + half_cells * offset_diff[1]
    step_z = coord_z + half_cells * offset_diff[2]
    inside = (
        (step_x >= 0)
        & (step_x < length)
        & (step_y >= 0)
        & (step_y < length)
        & (step_z >= 0)
        & (step_z < length)
    )
    shift_flat = half_cells * (
        offset_diff[0] * length * length + offset_diff[1] * length + offset_diff[2]
    )
    padded = jnp.pad(patch_flat, margin)
    start = margin + shift_flat
    moved = lax.dynamic_slice(padded, (start,), (volume,))
    return jnp.where(inside, moved, jnp.zeros_like(moved))


def pair_terms(first_patch, second_patch, offset_diff, live_mask, tables):
    table_x, table_yz, inverse = tables
    count = first_patch.shape[0]
    length = table_x.shape[0]
    moved = jax.vmap(lambda patch_flat, diff: move_flat(patch_flat, diff, length))(
        second_patch, offset_diff
    )
    moved = moved.reshape(count, length, length * length).astype(jnp.float32)
    density = first_patch.reshape(count, length, length * length).astype(jnp.float32) * moved
    potential = solve_box(density, table_x, table_yz, inverse)
    return (potential * moved * live_mask[:, None, None]).reshape(count, length**3)


def add_selected(totals, targets, terms):
    selector = (targets[None, :] == jnp.arange(totals.shape[0])[:, None]).astype(jnp.float32)
    return totals + jnp.dot(
        selector, terms, precision=lax.Precision.HIGHEST, preferred_element_type=jnp.float32
    )


def cube_root(volume):
    length = 1
    while length * length * length < volume:
        length = length + 1
    return length


def on_device(phi, offsets, fetch, task_pairs, task_count):
    node_count = lax.axis_size("orb")
    orb_local = phi.shape[0]
    volume = phi.shape[1]
    task_local = task_pairs.shape[0]
    length = cube_root(volume)
    asked_rows = lax.all_to_all(
        fetch.reshape(node_count, 1), "orb", split_axis=0, concat_axis=0, tiled=True
    )
    wanted = asked_rows[:, 0]
    picked = jnp.take(phi, jnp.maximum(wanted, 0), axis=0)
    outgoing = jnp.where((wanted >= 0)[:, None], picked, jnp.zeros_like(picked))
    incoming = lax.all_to_all(outgoing, "orb", split_axis=0, concat_axis=0, tiled=True)
    table_x = sine_table(length)
    tables = (table_x, jnp.kron(table_x, table_x), inverse_eigen(length))
    fetch_row = jnp.maximum(fetch[0], 0)
    slot_ids = jnp.arange(node_count) * orb_local + fetch_row
    slot_offsets = jnp.take(offsets, slot_ids, axis=0)

    def run_block(counter, partial_value):
        slot_rows = lax.dynamic_slice_in_dim(task_pairs, counter * task_batch, task_batch, 0)
        first_slot = slot_rows[:, 0]
        second_slot = slot_rows[:, 1]
        places = counter * task_batch + jnp.arange(task_batch)
        live_mask = (places < task_count[0]).astype(jnp.float32)
        offset_diff = slot_offsets[first_slot] - slot_offsets[second_slot]
        pair_sum = pair_terms(
            incoming[first_slot], incoming[second_slot], offset_diff, live_mask, tables
        )
        return add_selected(partial_value, first_slot, pair_sum)

    blocks = task_local // task_batch
    partial_value = lax.fori_loop(
        0, blocks, run_block, jnp.zeros((node_count, volume), jnp.float32)
    )
    returned = lax.all_to_all(partial_value, "orb", split_axis=0, concat_axis=0, tiled=True)
    selector = (wanted[:, None] == jnp.arange(orb_local)[None, :]).astype(jnp.float32)
    result = jnp.dot(
        selector.T, returned, precision=lax.Precision.HIGHEST, preferred_element_type=jnp.float32
    )
    return result


def solution(mesh):
    in_specs = (
        P(("groups", "orb"), None),
        P("groups", None),
        P(("groups", "orb"), None),
        P(("groups", "orb"), None),
        P(("groups", "orb")),
    )
    out_specs = P(("groups", "orb"), None)
    return jax.shard_map(
        on_device, mesh=mesh, in_specs=in_specs, out_specs=out_specs, check_vma=False
    )
```

profile of v0, /device:TPU:0, one launch (start us, length us, event | category | flops | bytes accessed | tf_op | source)
XLA Modules:
  0.0 685.0 jit_solution(15867317233733871790)
XLA Ops:
  0.8 13.6 %all_to_all.30 = s32[16,1,1]{2,1,0:T(1,128)S(1)} all-to-all(s32[16,1,1]{2,1,0:T(1,128)S(1)} %copy.18), channel_id=1, replica_groups=mesh['groups'=2,'orb'=16] {'orb'}, dimensions={0} | all-to-all | bytes 128 | tf_op jit(solution)/shard_map/all_to_all | solution.py:93
  20.1 3.7 all-to-all-start.1
  24.9 21.8 %all-to-all-done.1 = bf16[16,2,16384]{2,1,0:T(2,128)(2,1)S(1)} async-done(((bf16[16,2,16384]{2,1,0:T(2,128)(2,1)}), bf16[16,2,16384]{2,1,0:T(2,128)(2,1)S(1)}, u32[]{:S(2)}, u32[]{:S(2)}) %all-to-all-start.1) | async-done | bytes 1048608 | tf_op jit(solution)/shard_map/all_to_all | solution.py:99
  52.9 570.7 %while.23 = (s32[]{:T(128)}, f32[16,32768]{1,0:T(8,128)}, s32[48,2]{0,1:T(2,128)S(1)}, bf16[16,32768]{1,0:T(8,128)(2,1)S(1)}, s32[16,3]{1,0:T(8,128)S(1)}, /*ind...) while((s32[]{:T(128)}, f32[16,32768]{1,0:T(8,128)}, ...), condition=%wide.region_1.2_spmd.clone.clone, body=%wide.region_0.1_spmd.clone.clone.sunk | while | flops 6707355648 | bytes 63868584 | solution.py:119
  58.0 45.6 %while.24 = (s32[]{:T(128)}, bf16[8,66592]{1,0:T(8,128)(2,1)S(1)}, s32[8,2]{0,1:T(2,128)S(1)}, bf16[8,32768]{1,0:T(8,128)(2,1)}, s32[]{:T(128)}, /*index=5*/s32[]{:T(128)}) while((s32[]{:T(128)}, bf16[8,66592]{1,0:T(8,128)(2,1)S(1)}, s32[8,2]{0,1:T(2,128)S(1)}, bf16[8,32768]{1,0:T(8,128)(2,1)}, s32[]{:T(128)}, /*index=5*/s32[]{:T(128)}) %tuple.87), condition=%wide.while_cond, body=%wide.while_body.sunk | while | flops 2 | bytes 262257 | solution.py:56
  104.8 4.4 convolution_bitcast_fusion.4
  109.2 8.0 %broadcast_multiply_fusion.3 = f32[32,32,32,32]{3,2,1,0:T(8,128)} fusion(f32[32,32]{1,0:T(8,128)S(1)} %get-tuple-element.647), kind=kLoop, calls=%fused_computation.11.clone.1 | loop fusion | flops 1048576 | bytes 4198400 | tf_op jit(solution)/shard_map/jit(kron)/mul | solution.py:101
  117.1 13.7 %reshape.499 = f32[1024,1024,1]{1,0,2:T(8,128)} reshape(f32[32,32,32,32]{3,2,1,0:T(8,128)} %broadcast_multiply_fusion.3) | data formatting | bytes 8388608 | tf_op jit(solution)/shard_map/jit(kron)/mul | solution.py:101
  131.3 6.2 convolution_multiply_fusion.3
  139.3 4.6 fusion.74
  151.8 45.6 %while.24 = (s32[]{:T(128)}, bf16[8,66592]{1,0:T(8,128)(2,1)S(1)}, s32[8,2]{0,1:T(2,128)S(1)}, bf16[8,32768]{1,0:T(8,128)(2,1)}, s32[]{:T(128)}, /*index=5*/s32[]{:T(128)}) while((s32[]{:T(128)}, bf16[8,66592]{1,0:T(8,128)(2,1)S(1)}, s32[8,2]{0,1:T(2,128)S(1)}, bf16[8,32768]{1,0:T(8,128)(2,1)}, s32[]{:T(128)}, /*index=5*/s32[]{:T(128)}) %tuple.87), condition=%wide.while_cond, body=%wide.while_body.sunk | while | flops 2 | bytes 262257 | solution.py:56
  198.6 4.4 convolution_bitcast_fusion.4
  202.9 8.0 %broadcast_multiply_fusion.3 = f32[32,32,32,32]{3,2,1,0:T(8,128)} fusion(f32[32,32]{1,0:T(8,128)S(1)} %get-tuple-element.647), kind=kLoop, calls=%fused_computation.11.clone.1 | loop fusion | flops 1048576 | bytes 4198400 | tf_op jit(solution)/shard_map/jit(kron)/mul | solution.py:101
  210.9 13.7 %reshape.499 = f32[1024,1024,1]{1,0,2:T(8,128)} reshape(f32[32,32,32,32]{3,2,1,0:T(8,128)} %broadcast_multiply_fusion.3) | data formatting | bytes 8388608 | tf_op jit(solution)/shard_map/jit(kron)/mul | solution.py:101
  225.0 6.2 convolution_multiply_fusion.3
  233.1 4.6 fusion.74
  238.3 3.9 convolution_add_fusion.2
  247.1 45.6 %while.24 = (s32[]{:T(128)}, bf16[8,66592]{1,0:T(8,128)(2,1)S(1)}, s32[8,2]{0,1:T(2,128)S(1)}, bf16[8,32768]{1,0:T(8,128)(2,1)}, s32[]{:T(128)}, /*index=5*/s32[]{:T(128)}) while((s32[]{:T(128)}, bf16[8,66592]{1,0:T(8,128)(2,1)S(1)}, s32[8,2]{0,1:T(2,128)S(1)}, bf16[8,32768]{1,0:T(8,128)(2,1)}, s32[]{:T(128)}, /*index=5*/s32[]{:T(128)}) %tuple.87), condition=%wide.while_cond, body=%wide.while_body.sunk | while | flops 2 | bytes 262257 | solution.py:56
  293.9 4.4 convolution_bitcast_fusion.4
  298.3 8.0 %broadcast_multiply_fusion.3 = f32[32,32,32,32]{3,2,1,0:T(8,128)} fusion(f32[32,32]{1,0:T(8,128)S(1)} %get-tuple-element.647), kind=kLoop, calls=%fused_computation.11.clone.1 | loop fusion | flops 1048576 | bytes 4198400 | tf_op jit(solution)/shard_map/jit(kron)/mul | solution.py:101
  306.2 13.7 %reshape.499 = f32[1024,1024,1]{1,0,2:T(8,128)} reshape(f32[32,32,32,32]{3,2,1,0:T(8,128)} %broadcast_multiply_fusion.3) | data formatting | bytes 8388608 | tf_op jit(solution)/shard_map/jit(kron)/mul | solution.py:101
  320.4 6.2 convolution_multiply_fusion.3
  328.4 4.6 fusion.74
  333.6 3.9 convolution_add_fusion.2
  342.4 45.6 %while.24 = (s32[]{:T(128)}, bf16[8,66592]{1,0:T(8,128)(2,1)S(1)}, s32[8,2]{0,1:T(2,128)S(1)}, bf16[8,32768]{1,0:T(8,128)(2,1)}, s32[]{:T(128)}, /*index=5*/s32[]{:T(128)}) while((s32[]{:T(128)}, bf16[8,66592]{1,0:T(8,128)(2,1)S(1)}, s32[8,2]{0,1:T(2,128)S(1)}, bf16[8,32768]{1,0:T(8,128)(2,1)}, s32[]{:T(128)}, /*index=5*/s32[]{:T(128)}) %tuple.87), condition=%wide.while_cond, body=%wide.while_body.sunk | while | flops 2 | bytes 262257 | solution.py:56
  389.3 4.4 convolution_bitcast_fusion.4
  393.6 8.0 %broadcast_multiply_fusion.3 = f32[32,32,32,32]{3,2,1,0:T(8,128)} fusion(f32[32,32]{1,0:T(8,128)S(1)} %get-tuple-element.647), kind=kLoop, calls=%fused_computation.11.clone.1 | loop fusion | flops 1048576 | bytes 4198400 | tf_op jit(solution)/shard_map/jit(kron)/mul | solution.py:101
  401.6 13.7 %reshape.499 = f32[1024,1024,1]{1,0,2:T(8,128)} reshape(f32[32,32,32,32]{3,2,1,0:T(8,128)} %broadcast_multiply_fusion.3) | data formatting | bytes 8388608 | tf_op jit(solution)/shard_map/jit(kron)/mul | solution.py:101
  415.7 6.2 convolution_multiply_fusion.3
  423.7 4.6 fusion.74
  429.0 3.9 convolution_add_fusion.2
  437.8 45.6 %while.24 = (s32[]{:T(128)}, bf16[8,66592]{1,0:T(8,128)(2,1)S(1)}, s32[8,2]{0,1:T(2,128)S(1)}, bf16[8,32768]{1,0:T(8,128)(2,1)}, s32[]{:T(128)}, /*index=5*/s32[]{:T(128)}) while((s32[]{:T(128)}, bf16[8,66592]{1,0:T(8,128)(2,1)S(1)}, s32[8,2]{0,1:T(2,128)S(1)}, bf16[8,32768]{1,0:T(8,128)(2,1)}, s32[]{:T(128)}, /*index=5*/s32[]{:T(128)}) %tuple.87), condition=%wide.while_cond, body=%wide.while_body.sunk | while | flops 2 | bytes 262257 | solution.py:56
  484.6 4.4 convolution_bitcast_fusion.4
  489.0 8.0 %broadcast_multiply_fusion.3 = f32[32,32,32,32]{3,2,1,0:T(8,128)} fusion(f32[32,32]{1,0:T(8,128)S(1)} %get-tuple-element.647), kind=kLoop, calls=%fused_computation.11.clone.1 | loop fusion | flops 1048576 | bytes 4198400 | tf_op jit(solution)/shard_map/jit(kron)/mul | solution.py:101
  496.9 13.7 %reshape.499 = f32[1024,1024,1]{1,0,2:T(8,128)} reshape(f32[32,32,32,32]{3,2,1,0:T(8,128)} %broadcast_multiply_fusion.3) | data formatting | bytes 8388608 | tf_op jit(solution)/shard_map/jit(kron)/mul | solution.py:101
  511.1 6.2 convolution_multiply_fusion.3
  519.1 4.6 fusion.74
  524.3 3.9 convolution_add_fusion.2
  533.1 45.6 %while.24 = (s32[]{:T(128)}, bf16[8,66592]{1,0:T(8,128)(2,1)S(1)}, s32[8,2]{0,1:T(2,128)S(1)}, bf16[8,32768]{1,0:T(8,128)(2,1)}, s32[]{:T(128)}, /*index=5*/s32[]{:T(128)}) while((s32[]{:T(128)}, bf16[8,66592]{1,0:T(8,128)(2,1)S(1)}, s32[8,2]{0,1:T(2,128)S(1)}, bf16[8,32768]{1,0:T(8,128)(2,1)}, s32[]{:T(128)}, /*index=5*/s32[]{:T(128)}) %tuple.87), condition=%wide.while_cond, body=%wide.while_body.sunk | while | flops 2 | bytes 262257 | solution.py:56
  579.9 4.4 convolution_bitcast_fusion.4
  584.3 8.0 %broadcast_multiply_fusion.3 = f32[32,32,32,32]{3,2,1,0:T(8,128)} fusion(f32[32,32]{1,0:T(8,128)S(1)} %get-tuple-element.647), kind=kLoop, calls=%fused_computation.11.clone.1 | loop fusion | flops 1048576 | bytes 4198400 | tf_op jit(solution)/shard_map/jit(kron)/mul | solution.py:101
  592.3 13.7 %reshape.499 = f32[1024,1024,1]{1,0,2:T(8,128)} reshape(f32[32,32,32,32]{3,2,1,0:T(8,128)} %broadcast_multiply_fusion.3) | data formatting | bytes 8388608 | tf_op jit(solution)/shard_map/jit(kron)/mul | solution.py:101
  606.4 6.2 convolution_multiply_fusion.3
  614.4 4.6 fusion.74
  619.6 3.9 convolution_add_fusion.2
  623.6 3.7 all_to_all.24
  627.3 54.0 %all_to_all.31 = f32[16,1,32768]{2,1,0:T(1,128)S(1)} all-to-all(f32[16,1,32768]{2,1,0:T(1,128)S(1)} %all_to_all.24), channel_id=1, replica_groups=mesh['groups'=2,'orb'=16] {'orb'}, dimensions={0} | all-to-all | bytes 4194304 | tf_op jit(solution)/shard_map/all_to_all | solution.py:122
  681.3 3.7 fusion.38
  (409 shorter events, 342.8 us)
Async XLA Ops:
  0.0 15.1 %copy-start = (bf16[16,32768]{1,0:T(8,128)(2,1)S(1)}, bf16[16,32768]{1,0:T(8,128)(2,1)}, u32[]{:S(2)}) copy-start(bf16[16,32768]{1,0:T(8,128)(2,1)} %param.7) | copy-start | bytes 3145732
  18.5 5.3 copy-start.4
  18.5 5.4 copy-start.5
  20.1 26.6 %all-to-all-start.1 = ((bf16[16,2,16384]{2,1,0:T(2,128)(2,1)}), bf16[16,2,16384]{2,1,0:T(2,128)(2,1)S(1)}, u32[]{:S(2)}, u32[]{:S(2)}) async-start(bf16[16,2,16384]{2,1,0:T(2,128)(2,1)} %reshape.480), calls=%async_computation.1 | async-start | bytes 2097152 | tf_op jit(solution)/shard_map/all_to_all | solution.py:99
  50.1 2.8 copy-start.3
  131.3 8.0 %copy-start.1 = (f32[1024,1024,1]{1,0,2:T(8,128)S(1)}, f32[1024,1024,1]{1,0,2:T(8,128)}, u32[]{:S(2)}) copy-start(f32[1024,1024,1]{1,0,2:T(8,128)} %reshape.499) | copy-start | bytes 12582916 | tf_op jit(solution)/shard_map/while
  137.5 1.8 copy-start.2
  225.0 8.0 %copy-start.1 = (f32[1024,1024,1]{1,0,2:T(8,128)S(1)}, f32[1024,1024,1]{1,0,2:T(8,128)}, u32[]{:S(2)}) copy-start(f32[1024,1024,1]{1,0,2:T(8,128)} %reshape.499) | copy-start | bytes 12582916 | tf_op jit(solution)/shard_map/while
  231.2 1.8 copy-start.2
  320.4 8.0 %copy-start.1 = (f32[1024,1024,1]{1,0,2:T(8,128)S(1)}, f32[1024,1024,1]{1,0,2:T(8,128)}, u32[]{:S(2)}) copy-start(f32[1024,1024,1]{1,0,2:T(8,128)} %reshape.499) | copy-start | bytes 12582916 | tf_op jit(solution)/shard_map/while
  326.6 1.8 copy-start.2
  415.7 8.0 %copy-start.1 = (f32[1024,1024,1]{1,0,2:T(8,128)S(1)}, f32[1024,1024,1]{1,0,2:T(8,128)}, u32[]{:S(2)}) copy-start(f32[1024,1024,1]{1,0,2:T(8,128)} %reshape.499) | copy-start | bytes 12582916 | tf_op jit(solution)/shard_map/while
  421.9 1.8 copy-start.2
  511.1 8.0 %copy-start.1 = (f32[1024,1024,1]{1,0,2:T(8,128)S(1)}, f32[1024,1024,1]{1,0,2:T(8,128)}, u32[]{:S(2)}) copy-start(f32[1024,1024,1]{1,0,2:T(8,128)} %reshape.499) | copy-start | bytes 12582916 | tf_op jit(solution)/shard_map/while
  517.2 1.8 copy-start.2
  606.4 8.0 %copy-start.1 = (f32[1024,1024,1]{1,0,2:T(8,128)S(1)}, f32[1024,1024,1]{1,0,2:T(8,128)}, u32[]{:S(2)}) copy-start(f32[1024,1024,1]{1,0,2:T(8,128)} %reshape.499) | copy-start | bytes 12582916 | tf_op jit(solution)/shard_map/while
  612.6 1.8 copy-start.2
where the time goes:
time: 691 us; the launch traced here: 685 us
  local copies, waits for them, and re-layouts  407 us (59%)
  matrix products  123 us (18%)
  blocking collectives  67.6 us (10%)
  other arithmetic  60.2 us (9%)
  waiting for transfers between devices  21.8 us (3%)
    gather x192, local copies, waits for them, and re-layouts  273 us
    mul x6, local copies, waits for them, and re-layouts, on_device(): tables = (table_x, jnp.kron(table_x, table_x), inverse_eigen(length))  82.1 us
    all_to_all x1, blocking collectives, on_device(): lax.all_to_all(partial_value, 'orb', split_axis=0, concat_axis=0, tiled=T...  54 us
    mul x6, other arithmetic, on_device(): tables = (table_x, jnp.kron(table_x, table_x), inverse_eigen(length))  47.8 us
    dot_general x6, matrix products, solve_box(): spectrum = jnp.einsum('bkm,nm->bkn', spectrum, table_yz, precision=highest)  37 us
    dot_general x6, matrix products, solve_box(): return jnp.einsum('bkm,nm->bkn', potential, table_yz, precision=highest)  27.5 us
    dot_general x6, matrix products, solve_box(): spectrum = jnp.einsum('kx,bxm->bkm', table_x, density, precision=highest)  26.2 us
    dot_general x6, matrix products, add_selected(): jnp.dot(selector, terms, precision=lax.Precision.HIGHEST, preferred_eleme...  22.1 us
  transfers between devices with their start and end apart: 1, of which 1 were waited for; matrix products, arithmetic and copies ran while one was open for 0% of the time, Pallas kernels for 0%

commit v1 on v0

v1 whole, which is shorter than its diff:
```python
import functools

import jax
import jax.numpy as jnp
import ml_dtypes
import numpy as np
from jax import lax
from jax.experimental import pallas as pl
from jax.experimental.pallas import tpu as pltpu
from jax.sharding import PartitionSpec as P

BLOCK = 8
LEVELS = 32704.0
BF16 = jnp.bfloat16
F32 = jnp.float32


def cube_root(volume):
    length = 1
    while length * length * length < volume:
        length = length + 1
    return length


def split_bf16(values):
    high = values.astype(ml_dtypes.bfloat16)
    low = (values - high.astype(np.float64)).astype(ml_dtypes.bfloat16)
    return high, low


def host_tables(length):
    half = length // 2
    area = half * half
    count = np.arange(length) + 1.0
    sine = np.sqrt(2.0 / (length + 1)) * np.sin(np.pi * np.outer(count, count) / (length + 1))
    eigen = 2.0 - 2.0 * np.cos(np.pi * count / (length + 1))
    fold = [sine[parity::2, :half].T for parity in (0, 1)]
    forward, backward, factors = [], [], []
    for par_y in (0, 1):
        for par_z in (0, 1):
            table = np.kron(fold[par_y], fold[par_z])
            high, low = split_bf16(table)
            forward.append(np.concatenate([high, high, low], axis=0))
            high, low = split_bf16(table.T)
            backward.append(np.concatenate([high, high, low], axis=0))
            beta = 2.0 + (eigen[par_y::2][:, None] + eigen[par_z::2][None, :]).reshape(area)
            rows = [1.0 / beta]
            for _ in range(length - 1):
                rows.append(1.0 / (beta - rows[-1]))
            rows = np.stack(rows).astype(np.float32)
            factors.append(rows[:, : area // 2])
            factors.append(rows[:, area // 2 :])
    place = np.arange(area)
    low_y, low_z = place // half, place % half
    variants = []
    for rev_y, rev_z in ((0, 1), (1, 0), (1, 1)):
        src_y = half - 1 - low_y if rev_y else low_y
        src_z = half - 1 - low_z if rev_z else low_z
        one_hot = np.zeros((area, area), ml_dtypes.bfloat16)
        one_hot[src_y * half + src_z, place] = 1
        variants.append(one_hot)
    wide = 2 * area
    spot = np.arange(wide)
    pack = np.zeros((wide, wide), ml_dtypes.bfloat16)
    z_half, rest = spot // area, spot % area
    pack[(rest // half) * length + z_half * half + rest % half, spot] = 1
    unpack = []
    for par_y in (0, 1):
        y_nat = half - 1 - rest // half if par_y else rest // half
        z_nat = np.where(z_half == 1, length - 1 - rest % half, rest % half)
        one_hot = np.zeros((wide, wide), ml_dtypes.bfloat16)
        one_hot[spot, y_nat * length + z_nat] = 1
        unpack.append(one_hot)
    return dict(
        forward=np.stack(forward),
        backward=np.stack(backward),
        factors=np.stack(factors),
        variants=np.concatenate(variants, axis=1),
        pack=pack,
        unpack=np.stack(unpack),
    )


def halves(value):
    high = value.astype(BF16)
    low = (value - high.astype(F32)).astype(BF16)
    return high, low


def pack_kernel(phi_ref, table_ref, out_ref, work):
    orbs = phi_ref.shape[0]
    length = out_ref.shape[1]
    plane = length * length
    wide = plane // 2
    for y_half in range(2):
        rows = jnp.concatenate(
            [phi_ref[:, x * plane + y_half * wide : x * plane + (y_half + 1) * wide] for x in range(length)],
            axis=0,
        )
        moved = jnp.dot(rows, table_ref[...], preferred_element_type=F32)
        for j in range(wide // 128):
            work[y_half * (wide // 128) + j] = moved[:, j * 128 : (j + 1) * 128]
    for orb in range(orbs):
        for j in range(plane // 128):
            piece = work[j, pl.ds(orb, length, stride=orbs), :]
            out_ref[orb, :, j * 128 : (j + 1) * 128] = piece.astype(BF16)


def solve_kernel(
    orbs, fetch_ref, offsets_ref, pairs_ref, count_ref, in_ref, fwd_ref, bwd_ref, fac_ref, var_ref,
    out_ref, octs, grid_work, totals,
):
    nodes, length = in_ref.shape[0], in_ref.shape[1]
    half = length // 2
    area = half * half
    zero_at = nodes * 32
    octs[zero_at] = jnp.zeros((half, area), BF16)
    group = 8

    def make_variants(step, carry):
        for quad in range(4):
            block = in_ref[pl.ds(step * group, group), :, quad * area : (quad + 1) * area]
            turned = jnp.dot(
                block.reshape(group * length, area), var_ref[...], preferred_element_type=F32
            ).astype(BF16)
            for one in range(group):
                for hx in range(2):
                    base = (((step * group + one) * 2 + hx) * 4 + quad) * 4
                    octs[base] = block[one, hx * half : (hx + 1) * half]
                    first = one * length + hx * half
                    for rev in range(3):
                        octs[base + 1 + rev] = turned[first : first + half, rev * area : (rev + 1) * area]
        return carry

    lax.fori_loop(0, nodes // group, make_variants, 0)

    def clear(step, carry):
        totals[step] = jnp.zeros((half, area), F32)
        return carry

    lax.fori_loop(0, nodes * 8, clear, 0)
    live_count = count_ref[0]
    last_slot = pairs_ref.shape[0] // 2 - 1

    def task(slot):
        at = jnp.minimum(slot, last_slot)
        first, second = pairs_ref[2 * at], pairs_ref[2 * at + 1]
        id_a = first * orbs + jnp.maximum(fetch_ref[first], 0)
        id_b = second * orbs + jnp.maximum(fetch_ref[second], 0)
        diff = [offsets_ref[id_a * 3 + k] - offsets_ref[id_b * 3 + k] for k in range(3)]
        return first, second, diff, slot < live_count

    def second_at(second, diff, live, hx, py, pz):
        sx, sy, sz = hx + diff[0], py + diff[1], pz + diff[2]
        inside = live & (sx >= 0) & (sx < 2) & (sy >= 0) & (sy < 2) & (sz >= 0) & (sz < 2)
        found = (((second * 2 + sx) * 2 + sy) * 2 + sz) * 4 + (py * 2 + pz)
        return jnp.where(inside, found, zero_at)

    def run_block(step, carry):
        places = []
        for t in range(BLOCK):
            first, second, diff, live = task(step * BLOCK + t)
            spots = [
                [second_at(second, diff, live, hx, py, pz) for py in range(2) for pz in range(2)]
                for hx in range(2)
            ]
            places.append((first, spots))
        for t in range(BLOCK):
            first, spots = places[t]
            for hx in range(2):
                dens = []
                for pos in range(4):
                    own = octs[((first * 2 + hx) * 4 + pos) * 4 + pos].astype(F32)
                    dens.append(own * octs[spots[hx][pos]].astype(F32))
                even0, odd0 = dens[0] + dens[1], dens[0] - dens[1]
                even1, odd1 = dens[2] + dens[3], dens[2] - dens[3]
                folded = (even0 + even1, odd0 + odd1, even0 - even1, odd0 - odd1)
                for cls in range(4):
                    for lh in range(2):
                        grid_work[cls * 2 + lh, pl.ds(hx * half * BLOCK + t, half, stride=BLOCK), :] = (
                            folded[cls][:, lh * 128 : (lh + 1) * 128]
                        )

        def transform(cls, table_ref):
            both = jnp.concatenate([grid_work[cls * 2], grid_work[cls * 2 + 1]], axis=1)
            high, low = halves(both)
            result = jnp.dot(
                jnp.concatenate([high, low, high], axis=1), table_ref[cls], preferred_element_type=F32
            )
            grid_work[cls * 2] = result[:, :128]
            grid_work[cls * 2 + 1] = result[:, 128:]

        for cls in range(4):
            transform(cls, fwd_ref)
        chains = range(8)
        run = [None] * 8
        for x in range(length):
            for ch in chains:
                here = grid_work[ch, x * BLOCK : (x + 1) * BLOCK, :]
                factor = jnp.broadcast_to(fac_ref[ch, x : x + 1, :], (BLOCK, 128))
                run[ch] = (here if x == 0 else here + run[ch]) * factor
                grid_work[ch, x * BLOCK : (x + 1) * BLOCK, :] = run[ch]
        for x in range(length - 2, -1, -1):
            for ch in chains:
                here = grid_work[ch, x * BLOCK : (x + 1) * BLOCK, :]
                factor = jnp.broadcast_to(fac_ref[ch, x : x + 1, :], (BLOCK, 128))
                run[ch] = here + factor * run[ch]
                grid_work[ch, x * BLOCK : (x + 1) * BLOCK, :] = run[ch]
        for cls in range(4):
            transform(cls, bwd_ref)
        for t in range(BLOCK):
            first, spots = places[t]
            for hx in range(2):
                folded = []
                for cls in range(4):
                    folded.append(
                        jnp.concatenate(
                            [
                                grid_work[cls * 2 + lh, pl.ds(hx * half * BLOCK + t, half, stride=BLOCK), :]
                                for lh in range(2)
                            ],
                            axis=1,
                        )
                    )
                sum0, dif0 = folded[0] + folded[1], folded[0] - folded[1]
                sum1, dif1 = folded[2] + folded[3], folded[2] - folded[3]
                potential = (sum0 + sum1, dif0 + dif1, sum0 - sum1, dif0 - dif1)
                for pos in range(4):
                    moved = octs[spots[hx][pos]].astype(F32)
                    totals[first * 8 + hx * 4 + pos] += potential[pos] * moved
        return carry

    lax.fori_loop(0, (live_count + BLOCK - 1) // BLOCK, run_block, 0)

    def send_out(owner, carry):
        top = jnp.abs(totals[owner * 8])
        for k in range(1, 8):
            top = jnp.maximum(top, jnp.abs(totals[owner * 8 + k]))
        top = jnp.maximum(jnp.max(top, axis=0, keepdims=True), 2.0**-110)
        power = jnp.ceil(jnp.log2(top) + 1e-4)
        gain = jnp.exp2(-power) * LEVELS
        for k in range(8):
            level = jnp.round(totals[owner * 8 + k] * gain).astype(jnp.int32).astype(jnp.int16)
            for lh in range(2):
                first = (k * 2 + lh) * half
                out_ref[owner, first : first + half, :] = level[:, lh * 128 : (lh + 1) * 128]
        codes = jnp.concatenate(
            [jnp.broadcast_to(power[:, lh * 128 : (lh + 1) * 128], (8, 128)) for lh in range(2)], axis=0
        )
        out_ref[owner, 16 * half :, :] = codes.astype(jnp.int32).astype(jnp.int16)
        return carry

    lax.fori_loop(0, nodes, send_out, 0)


def final_kernel(wanted_ref, in_ref, table_ref, out_ref, totals, work):
    nodes = in_ref.shape[0]
    orbs = out_ref.shape[0]
    length = work.shape[1] // orbs
    half = length // 2
    area = half * half
    plane = length * length
    totals[...] = jnp.zeros_like(totals)

    def add_one(node, carry):
        target = wanted_ref[node]

        @pl.when(target >= 0)
        def _():
            codes = in_ref[node, 16 * half :, :].astype(jnp.int32).astype(F32)
            for lh in range(2):
                gain = jnp.exp2(codes[lh * 8 : lh * 8 + 1]) * (1.0 / LEVELS)
                for k in range(8):
                    first = (k * 2 + lh) * half
                    level = in_ref[node, first : first + half, :].astype(jnp.int32).astype(F32)
                    hx, pos = k // 4, k % 4
                    totals[pos * 2 + lh, pl.ds(target * length + hx * half, half), :] += level * gain

        return carry

    lax.fori_loop(0, nodes, add_one, 0)
    for py in range(2):
        rows = jnp.concatenate([totals[py * 4 + j] for j in range(4)], axis=1)
        high, low = halves(rows)
        result = jnp.dot(high, table_ref[py], preferred_element_type=F32) + jnp.dot(
            low, table_ref[py], preferred_element_type=F32
        )
        for j in range(4):
            work[py * 4 + j] = result[:, j * 128 : (j + 1) * 128]
    for x in range(length):
        for j in range(plane // 128):
            out_ref[:, x * plane + j * 128 : x * plane + (j + 1) * 128] = work[
                j, pl.ds(x, orbs, stride=length), :
            ]


def on_device(phi, offsets, fetch, task_pairs, task_count):
    nodes = lax.axis_size("orb")
    orbs, volume = phi.shape
    length = cube_root(volume)
    half, plane = length // 2, length * length
    area = half * half
    tables = host_tables(length)
    smem = pl.BlockSpec(memory_space=pltpu.SMEM)
    vmem = pl.BlockSpec(memory_space=pltpu.VMEM)
    params = pltpu.CompilerParams(vmem_limit_bytes=56 << 20)
    packed = pl.pallas_call(
        pack_kernel,
        out_shape=jax.ShapeDtypeStruct((orbs, length, plane), BF16),
        in_specs=[vmem, vmem],
        out_specs=vmem,
        scratch_shapes=[pltpu.VMEM((plane // 128, orbs * length, 128), F32)],
        compiler_params=params,
        name="pack",
    )(phi, tables["pack"])
    asked = lax.all_to_all(fetch.reshape(nodes, 1), "orb", split_axis=0, concat_axis=0, tiled=True)
    wanted = asked[:, 0]
    outgoing = jnp.take(packed, jnp.maximum(wanted, 0), axis=0)
    incoming = lax.all_to_all(outgoing, "orb", split_axis=0, concat_axis=0, tiled=True)
    rows = 16 * half + 16
    partial = pl.pallas_call(
        functools.partial(solve_kernel, orbs),
        out_shape=jax.ShapeDtypeStruct((nodes, rows, 128), jnp.int16),
        in_specs=[smem] * 4 + [vmem] * 5,
        out_specs=vmem,
        scratch_shapes=[
            pltpu.VMEM((nodes * 32 + 1, half, area), BF16),
            pltpu.VMEM((8, length * BLOCK, 128), F32),
            pltpu.VMEM((nodes * 8, half, area), F32),
        ],
        compiler_params=params,
        name="solve",
    )(
        fetch.reshape(-1), offsets.reshape(-1), task_pairs.reshape(-1), task_count, incoming,
        tables["forward"], tables["backward"], tables["factors"], tables["variants"],
    )
    returned = lax.all_to_all(partial, "orb", split_axis=0, concat_axis=0, tiled=True)
    return pl.pallas_call(
        final_kernel,
        out_shape=jax.ShapeDtypeStruct((orbs, volume), F32),
        in_specs=[smem, vmem, vmem],
        out_specs=vmem,
        scratch_shapes=[
            pltpu.VMEM((8, orbs * length, 128), F32),
            pltpu.VMEM((plane // 128, orbs * length, 128), F32),
        ],
        compiler_params=params,
        name="final",
    )(wanted, returned, tables["unpack"])


def solution(mesh):
    in_specs = (
        P(("groups", "orb"), None),
        P("groups", None),
        P(("groups", "orb"), None),
        P(("groups", "orb"), None),
        P(("groups", "orb")),
    )
    out_specs = P(("groups", "orb"), None)
    return jax.shard_map(
        on_device, mesh=mesh, in_specs=in_specs, out_specs=out_specs, check_vma=False
    )
```

time: 691 us -> 106 us (0.15)
  local copies, waits for them, and re-layouts: 407 us -> 5.87 us
  matrix products: 123 us -> 0 us
  other arithmetic: 60.2 us -> 1.81 us
  blocking collectives: 67.6 us -> 35.4 us
  Pallas kernels: 0 us -> 27.8 us
  starting transfers between devices: 3.65 us -> 11.2 us
    gather x218 -> x1, local copies, waits for them, and re-layouts: 297 us -> 1.84 us  [on_device(): outgoing = jnp.take(packed, jnp.maximum(wanted, 0), axis=0)]
    dot_general x31 -> x0, matrix products: 123 us -> none  [the longest x6 37 us: solve_box(): spectrum = jnp.einsum('bkm,nm->bkn', spectrum, table_yz, precision=highest)]
    mul x12 -> x0, local copies, waits for them, and re-layouts: 83.5 us -> none  [the longest x6 82.1 us: on_device(): tables = (table_x, jnp.kron(table_x, table_x), inverse_eigen(length))]
    mul x13 -> x0, other arithmetic: 49 us -> none  [the longest x6 47.8 us: on_device(): tables = (table_x, jnp.kron(table_x, table_x), inverse_eigen(length))]
    all_to_all x2 -> x1, blocking collectives: 67.6 us -> 35.4 us  [on_device(): lax.all_to_all(partial, 'orb', split_axis=0, concat_axis=0, tiled=True)]
    pallas_call x0 -> x3, Pallas kernels: none -> 27.8 us  [the longest x1 17.8 us: on_device(): pl.pallas_call(functools.partial(solve_kernel, orbs), out_shape=jax.Shape...]
    pad x6 -> x0, local copies, waits for them, and re-layouts: 7.55 us -> none  [move_flat(): padded = jnp.pad(patch_flat, margin)]
    all_to_all x0 -> x1, starting transfers between devices: none -> 7.39 us  [on_device(): lax.all_to_all(fetch.reshape(nodes, 1), 'orb', split_axis=0, concat_axis=...]
  transfers between devices with their start and end apart: 1 -> 2, of which waited for: 1 -> 2; matrix products, arithmetic and copies ran while one was open for 0% -> 2% of each run, Pallas kernels for 0% -> 3%
where the time goes in v1:
time: 106 us
  blocking collectives  35.4 us (33%)
  Pallas kernels  27.8 us (26%)
  waiting for transfers between devices  23.2 us (22%)
  starting transfers between devices  11.2 us (11%)
  local copies, waits for them, and re-layouts  5.87 us (6%)
  other arithmetic  1.81 us (2%)
    all_to_all x1, blocking collectives, on_device(): lax.all_to_all(partial, 'orb', split_axis=0, concat_axis=0, tiled=True)  35.4 us
    all_to_all x1, waiting for transfers between devices, on_device(): lax.all_to_all(outgoing, 'orb', split_axis=0, concat_axis=0, tiled=True)  20.5 us
    pallas_call x1, Pallas kernels, on_device(): pl.pallas_call(functools.partial(solve_kernel, orbs), out_shape=jax.Shape...  17.8 us
    all_to_all x1, starting transfers between devices, on_device(): lax.all_to_all(fetch.reshape(nodes, 1), 'orb', split_axis=0, concat_axis=...  7.39 us
    pallas_call x1, Pallas kernels, on_device(): pl.pallas_call(final_kernel, out_shape=jax.ShapeDtypeStruct((orbs, volume...  6.3 us
    all_to_all x1, starting transfers between devices, on_device(): lax.all_to_all(outgoing, 'orb', split_axis=0, concat_axis=0, tiled=True)  3.79 us
    pallas_call x1, Pallas kernels, on_device(): pl.pallas_call(pack_kernel, out_shape=jax.ShapeDtypeStruct((orbs, length,...  3.69 us
    all_to_all x1, waiting for transfers between devices, on_device(): lax.all_to_all(fetch.reshape(nodes, 1), 'orb', split_axis=0, concat_axis=...  2.71 us
  transfers between devices with their start and end apart: 2, of which 2 were waited for; matrix products, arithmetic and copies ran while one was open for 2% of the time, Pallas kernels for 3%

profile of v1, /device:TPU:0, one launch (start us, length us, event | category | flops | bytes accessed | tf_op | source)
XLA Modules:
  0.0 106.0 jit_solution(17631362106269431295)
XLA Ops:
  0.0 1.3 %copy.18 = s32[16,1,1]{2,1,0:T(1,128)} copy(s32[16,1,1]{0,2,1:T(1,128)} %bitcast.2) | data formatting | bytes 128 | tf_op jit(solution)/shard_map/all_to_all | solution.py:316
  1.3 7.4 %all-to-all-start = ((s32[16,1,1]{2,1,0:T(1,128)}), s32[16,1,1]{2,1,0:T(1,128)S(1)}, u32[]{:S(2)}, u32[]{:S(2)}) async-start(s32[16,1,1]{2,1,0:T(1,128)} %copy.18), calls=%async_computation | async-start | bytes 16384 | tf_op jit(solution)/shard_map/all_to_all | solution.py:316
  8.7 3.7 %pack.1 = bf16[16,32,1024]{2,1,0:T(8,128)(2,1)} custom-call(bf16[16,32768]{1,0:T(8,128)(2,1)} %phi_ref.1, bf16[512,512]{1,0:T(8,128)(2,1)} %constant.30.clone.table_ref), custom_call_target="tpu_custom_call" | custom-call | tf_op jit(solution)/shard_map/pack/pallas_call | solution.py:307
  12.4 2.7 %all-to-all-done = s32[16,1,1]{2,1,0:T(1,128)S(1)} async-done(((s32[16,1,1]{2,1,0:T(1,128)}), s32[16,1,1]{2,1,0:T(1,128)S(1)}, u32[]{:S(2)}, u32[]{:S(2)}) %all-to-all-start) | async-done | bytes 96 | tf_op jit(solution)/shard_map/all_to_all | solution.py:316
  15.1 0.7 maximum_reduce_fusion
  15.8 0.0 copy-start.2
  15.8 1.8 %gather_fusion = bf16[16,32,1024]{2,1,0:T(8,128)(2,1)S(1)} fusion(bf16[16,32,1024]{2,1,0:T(8,128)(2,1)} %pack.1, s32[1024]{0:T(1024)S(1)} %pad_clamp_fusion), kind=kCustom, calls=%fused_computation | custom fusion | bytes 2097216 | tf_op jit(solution)/shard_map/jit(_take)/gather | solution.py:318
  17.7 1.1 %broadcast_select_fusion = bf16[16,32,1024]{2,1,0:T(8,128)(2,1)} fusion(bf16[16,32,1024]{2,1,0:T(8,128)(2,1)S(1)} %gather_fusion, pred[16]{0:T(512)(128)(4,1)S(1)} %maximum_compare_fusion), kind=kLoop, calls=%fused_computation.1 | loop fusion | flops 524288 | bytes 2097168 | tf_op jit(solution)/shard_map/jit(_take)/select_n | solution.py:318
  18.8 0.0 copy-done.2
  18.8 0.0 copy-start.3
  18.8 0.0 copy-start.1
  18.8 3.8 %all-to-all-start.1 = ((bf16[16,32,1024]{2,1,0:T(8,128)(2,1)}), bf16[16,32,1024]{2,1,0:T(8,128)(2,1)S(1)}, u32[]{:S(2)}, u32[]{:S(2)}) async-start(bf16[16,32,1024]{2,1,0:T(8,128)(2,1)} %broadcast_select_fusion), calls=%async_computation.1 | async-start | bytes 2097152 | tf_op jit(solution)/shard_map/all_to_all | solution.py:319
  23.3 0.0 copy-done.3
  23.3 0.1 copy.20
  23.4 0.7 reshape.32.pairs_ref
  24.1 0.0 copy-done.1
  24.1 0.1 copy.19
  24.2 0.8 reshape.31.offsets_ref
  25.0 20.5 %all-to-all-done.1.in_ref = bf16[16,32,1024]{2,1,0:T(8,128)(2,1)S(1)} async-done(((bf16[16,32,1024]{2,1,0:T(8,128)(2,1)}), bf16[16,32,1024]{2,1,0:T(8,128)(2,1)S(1)}, u32[]{:S(2)}, u32[]{:S(2)}) %all-to-all-start.1) | async-done | bytes 1048608 | tf_op jit(solution)/shard_map/all_to_all | solution.py:319
  45.5 0.0 copy-start
  45.5 1.0 copy-done
  46.5 17.8 %solve.1 = s16[16,272,128]{2,1,0:T(8,128)(2,1)} custom-call(s32[16]{0:T(128)} %bitcast.3, s32[768]{0:T(1024)} %reshape.31.offsets_ref, s32[96]{0:T(128)} %reshape.32.pairs_ref, s32[1]{0:T(128)S(6)} %copy.21.count_ref, bf16[16,32,1024]{2,1,0:T(8,128)(2,1)} %copy-done, bf16[4,768,256]{2,1,0:T(8,128)(2,1)} %constant.31.clone.fwd_ref, ...), custom_call_target="tpu_custom_call" | custom-call | tf_op jit(solution)/shard_map/solve/pallas_call | solution.py:321
  64.3 35.4 %all_to_all.19.in_ref = s16[16,272,128]{2,1,0:T(8,128)(2,1)} all-to-all(s16[16,272,128]{2,1,0:T(8,128)(2,1)} %solve.1), channel_id=1, replica_groups=mesh['groups'=2,'orb'=16] {'orb'}, dimensions={0} | all-to-all | bytes 2228224 | tf_op jit(solution)/shard_map/all_to_all | solution.py:337
  99.7 6.3 %final.1 = f32[16,32768]{1,0:T(8,128)} custom-call(s32[16]{0:T(128)} %copy-done.2, s16[16,272,128]{2,1,0:T(8,128)(2,1)} %all_to_all.19.in_ref, bf16[2,512,512]{2,1,0:T(8,128)(2,1)} %constant.35.clone.table_ref), custom_call_target="tpu_custom_call" | custom-call | tf_op jit(solution)/shard_map/final/pallas_call | solution.py:338
  (2 shorter events, 0.0 us)
Async XLA Ops:
  1.3 13.8 %all-to-all-start = ((s32[16,1,1]{2,1,0:T(1,128)}), s32[16,1,1]{2,1,0:T(1,128)S(1)}, u32[]{:S(2)}, u32[]{:S(2)}) async-start(s32[16,1,1]{2,1,0:T(1,128)} %copy.18), calls=%async_computation | async-start | bytes 16384 | tf_op jit(solution)/shard_map/all_to_all | solution.py:316
  15.8 3.0 %copy-start.2 = (s32[16]{0:T(128)}, s32[16]{0:T(128)S(1)}, u32[]{:S(2)}) copy-start(s32[16]{0:T(128)S(1)} %get-tuple-element.6.wanted_ref) | copy-start | bytes 196
  18.8 4.4 %copy-start.3 = (s32[48,2]{0,1:T(2,128)S(1)}, s32[48,2]{0,1:T(2,128)}, u32[]{:S(2)}) copy-start(s32[48,2]{0,1:T(2,128)} %param.14) | copy-start | bytes 1156
  18.8 5.3 %copy-start.1 = (s32[256,3]{0,1:T(4,128)S(1)}, s32[256,3]{0,1:T(4,128)}, u32[]{:S(2)}) copy-start(s32[256,3]{0,1:T(4,128)} %param.12) | copy-start | bytes 9220
  18.8 26.7 %all-to-all-start.1 = ((bf16[16,32,1024]{2,1,0:T(8,128)(2,1)}), bf16[16,32,1024]{2,1,0:T(8,128)(2,1)S(1)}, u32[]{:S(2)}, u32[]{:S(2)}) async-start(bf16[16,32,1024]{2,1,0:T(8,128)(2,1)} %broadcast_select_fusion), calls=%async_computation.1 | async-start | bytes 2097152 | tf_op jit(solution)/shard_map/all_to_all | solution.py:319
  45.5 1.0 copy-start

commit v2 on v1

v2 whole, which is shorter than its diff:
```python
import functools

import jax
import jax.numpy as jnp
import ml_dtypes
import numpy as np
from jax import lax
from jax.experimental import pallas as pl
from jax.experimental.pallas import tpu as pltpu
from jax.sharding import PartitionSpec as P

BLOCK = 8
PITCH = 9
LEVELS = 32704.0
BF16 = jnp.bfloat16
F32 = jnp.float32


def cube_root(volume):
    length = 1
    while length * length * length < volume:
        length = length + 1
    return length


def split_bf16(values):
    high = values.astype(ml_dtypes.bfloat16)
    low = (values - high.astype(np.float64)).astype(ml_dtypes.bfloat16)
    return high, low


def host_tables(length):
    half = length // 2
    area = half * half
    count = np.arange(length) + 1.0
    sine = np.sqrt(2.0 / (length + 1)) * np.sin(np.pi * np.outer(count, count) / (length + 1))
    eigen = 2.0 - 2.0 * np.cos(np.pi * count / (length + 1))
    fold = [sine[parity::2, :half].T for parity in (0, 1)]
    forward, backward, factors = [], [], []
    for par_y in (0, 1):
        for par_z in (0, 1):
            table = np.kron(fold[par_y], fold[par_z])
            high, low = split_bf16(table)
            forward.append(np.concatenate([high, high, low], axis=0))
            high, low = split_bf16(table.T)
            backward.append(np.concatenate([high, high, low], axis=0))
            beta = 2.0 + (eigen[par_y::2][:, None] + eigen[par_z::2][None, :]).reshape(area)
            rows = [1.0 / beta]
            for _ in range(half - 1):
                rows.append(1.0 / (beta - rows[-1]))
            rows.append(1.0 / (1.0 - rows[-1] ** 2))
            rows.extend([rows[-1]] * 7)
            rows = np.stack(rows).astype(np.float32)
            factors.append(rows[:, : area // 2])
            factors.append(rows[:, area // 2 :])
    place = np.arange(area)
    low_y, low_z = place // half, place % half
    variants = []
    for rev_y, rev_z in ((0, 1), (1, 0), (1, 1)):
        src_y = half - 1 - low_y if rev_y else low_y
        src_z = half - 1 - low_z if rev_z else low_z
        one_hot = np.zeros((area, area), ml_dtypes.bfloat16)
        one_hot[src_y * half + src_z, place] = 1
        variants.append(one_hot)
    wide = 2 * area
    spot = np.arange(wide)
    pack = np.zeros((wide, wide), ml_dtypes.bfloat16)
    z_half, rest = spot // area, spot % area
    pack[(rest // half) * length + z_half * half + rest % half, spot] = 1
    unpack = []
    for par_y in (0, 1):
        y_nat = half - 1 - rest // half if par_y else rest // half
        z_nat = np.where(z_half == 1, length - 1 - rest % half, rest % half)
        one_hot = np.zeros((wide, wide), ml_dtypes.bfloat16)
        one_hot[spot, y_nat * length + z_nat] = 1
        unpack.append(one_hot)
    return dict(
        forward=np.stack(forward),
        backward=np.stack(backward),
        factors=np.stack(factors),
        variants=np.concatenate(variants, axis=1),
        pack=pack,
        unpack=np.stack(unpack),
    )


def halves(value):
    high = value.astype(BF16)
    low = (value - high.astype(F32)).astype(BF16)
    return high, low


def ask_kernel(fetch_ref, out_ref):
    for node in range(out_ref.shape[0]):
        out_ref[node] = jnp.full(out_ref.shape[1:], fetch_ref[node], jnp.int32)


def pack_kernel(phi_ref, table_ref, out_ref, work):
    orbs = phi_ref.shape[0]
    length = out_ref.shape[1]
    plane = length * length
    wide = plane // 2
    pitch = orbs + 1
    for y_half in range(2):
        rows = jnp.concatenate(
            [phi_ref[:, x * plane + y_half * wide : x * plane + (y_half + 1) * wide] for x in range(length)],
            axis=0,
        )
        moved = jnp.dot(rows, table_ref[...], preferred_element_type=F32)
        for j in range(wide // 128):
            for x in range(length):
                work[y_half * (wide // 128) + j, x * pitch : x * pitch + orbs, :] = moved[
                    x * orbs : (x + 1) * orbs, j * 128 : (j + 1) * 128
                ]
    for orb in range(orbs):
        for j in range(plane // 128):
            piece = work[j, pl.ds(orb, length, stride=pitch), :]
            out_ref[orb, :, j * 128 : (j + 1) * 128] = piece.astype(BF16)


def pick_kernel(asked_ref, packed_ref, out_ref, sems):
    nodes = out_ref.shape[0]
    copies = []
    for node in range(nodes):
        orb = jnp.maximum(asked_ref[node, 0, 0], 0)
        copies.append(pltpu.make_async_copy(packed_ref.at[orb], out_ref.at[node], sems.at[node]))
        copies[-1].start()
    for copy in copies:
        copy.wait()


def solve_kernel(
    orbs, fetch_ref, offsets_ref, pairs_ref, count_ref, in_hbm, var_hbm, fwd_hbm, bwd_hbm, fac_hbm,
    out_hbm, octs, even_work, odd_work, totals, plan, fwd_ref, bwd_ref, fac_ref, var_ref, in_ref,
    out_ref, sems, in_sems, out_sems,
):
    nodes, length = in_ref.shape[0], in_ref.shape[1]
    half = length // 2
    area = half * half
    zero_at = nodes * 32
    group = 8
    sources = ((var_hbm, var_ref), (fwd_hbm, fwd_ref), (bwd_hbm, bwd_ref), (fac_hbm, fac_ref))
    tables = [
        pltpu.make_async_copy(source, target, sems.at[k]) for k, (source, target) in enumerate(sources)
    ]
    def arrival(step):
        spots = pl.ds(step * group, group)
        return pltpu.make_async_copy(in_hbm.at[spots], in_ref.at[spots], in_sems.at[step])

    tables[0].start()
    for step in range(nodes // group):
        arrival(step).start()
    for table in tables[1:]:
        table.start()
    octs[zero_at] = jnp.zeros((half, area), BF16)
    live_count = count_ref[0]
    last_slot = pairs_ref.shape[0] // 2 - 1

    def make_variants(step, carry):
        arrival(step).wait()
        for quad in range(4):
            block = in_ref[pl.ds(step * group, group), :, quad * area : (quad + 1) * area]
            turned = jnp.dot(
                block.reshape(group * length, area), var_ref[...], preferred_element_type=F32
            ).astype(BF16)
            for one in range(group):
                for hx in range(2):
                    base = (((step * group + one) * 2 + hx) * 4 + quad) * 4
                    octs[base] = block[one, hx * half : (hx + 1) * half]
                    first = one * length + hx * half
                    for rev in range(3):
                        octs[base + 1 + rev] = turned[first : first + half, rev * area : (rev + 1) * area]
        return carry

    tables[0].wait()
    lax.fori_loop(0, nodes // group, make_variants, 0)

    def clear(step, carry):
        for k in range(8):
            totals[step * 8 + k] = jnp.zeros((half, area), F32)
        return carry

    lax.fori_loop(0, nodes, clear, 0)
    for ch in range(8):
        even_work[ch] = jnp.zeros(even_work.shape[1:], F32)
        odd_work[ch] = jnp.zeros(odd_work.shape[1:], F32)
    for t in range(BLOCK):
        plan[t * 9] = 0
        for k in range(8):
            plan[t * 9 + 1 + k] = zero_at

    def multiply(work, slot, t):
        at = jnp.minimum(slot, last_slot)
        first, second = pairs_ref[2 * at], pairs_ref[2 * at + 1]
        id_a = first * orbs + jnp.maximum(fetch_ref[first], 0)
        id_b = second * orbs + jnp.maximum(fetch_ref[second], 0)
        shift = [offsets_ref[id_a * 3 + k] - offsets_ref[id_b * 3 + k] for k in range(3)]
        fits = [[(side + shift[k] >= 0) & (side + shift[k] < 2) for side in range(2)] for k in range(3)]
        start = second * 32 + shift[0] * 16 + shift[1] * 8 + shift[2] * 4
        live = slot < live_count
        note = (slot + BLOCK) * 9
        plan[note] = first
        for hx in range(2):
            dens = []
            for pos in range(4):
                py, pz = pos // 2, pos % 2
                inside = live & fits[0][hx] & fits[1][py] & fits[2][pz]
                spot = jnp.where(inside, start + (hx * 16 + py * 8 + pz * 4 + pos), zero_at)
                plan[note + 1 + hx * 4 + pos] = spot
                own = octs[first * 32 + (hx * 16 + pos * 5)].astype(F32)
                dens.append(own * octs[spot].astype(F32))
            even0, odd0 = dens[0] + dens[1], dens[0] - dens[1]
            even1, odd1 = dens[2] + dens[3], dens[2] - dens[3]
            folded = (even0 + even1, odd0 + odd1, even0 - even1, odd0 - odd1)
            for cls in range(4):
                for lh in range(2):
                    work[cls * 2 + lh, pl.ds(hx * half * PITCH + t, half, stride=PITCH), :] = folded[cls][
                        :, lh * 128 : (lh + 1) * 128
                    ]

    def gather(work, slot, t):
        note = (slot + BLOCK) * 9
        first = plan[note] * 8
        for hx in range(2):
            folded = []
            for cls in range(4):
                pieces = [
                    work[cls * 2 + lh, pl.ds(hx * half * PITCH + t, half, stride=PITCH), :] for lh in range(2)
                ]
                folded.append(jnp.concatenate(pieces, axis=1))
            sum0, dif0 = folded[0] + folded[1], folded[0] - folded[1]
            sum1, dif1 = folded[2] + folded[3], folded[2] - folded[3]
            potential = (sum0 + sum1, dif0 + dif1, sum0 - sum1, dif0 - dif1)
            for pos in range(4):
                moved = octs[plan[note + 1 + hx * 4 + pos]].astype(F32)
                totals[first + (hx * 4 + pos)] += potential[pos] * moved

    def begin(work, cls, table_ref):
        both = jnp.concatenate(
            [
                jnp.concatenate(
                    [work[cls * 2 + lh, x * PITCH : x * PITCH + BLOCK, :] for x in range(length)], axis=0
                )
                for lh in range(2)
            ],
            axis=1,
        )
        high, low = halves(both)
        return jnp.dot(
            jnp.concatenate([high, low, high], axis=1), table_ref[cls], preferred_element_type=F32
        )

    def finish(work, cls, result):
        for x in range(length):
            for lh in range(2):
                work[cls * 2 + lh, x * PITCH : x * PITCH + BLOCK, :] = result[
                    x * BLOCK : (x + 1) * BLOCK, lh * 128 : (lh + 1) * 128
                ]

    def sweep(work, chains):
        def rows(x):
            return slice(x * PITCH, x * PITCH + BLOCK)

        def factor(ch, x):
            return jnp.broadcast_to(fac_ref[ch, x : x + 1, :], (BLOCK, 128))

        low, high = {}, {}
        for x in range(half):
            far = length - 1 - x
            for ch in chains:
                scale = factor(ch, x)
                from_low, from_high = work[ch, rows(x), :], work[ch, rows(far), :]
                if x > 0:
                    from_low, from_high = from_low + low[ch], from_high + high[ch]
                low[ch], high[ch] = from_low * scale, from_high * scale
                if x < half - 1:
                    work[ch, rows(x), :] = low[ch]
                    work[ch, rows(far), :] = high[ch]
        for ch in chains:
            scale, meet = factor(ch, half - 1), factor(ch, half)
            low[ch], high[ch] = (low[ch] + scale * high[ch]) * meet, (high[ch] + scale * low[ch]) * meet
            work[ch, rows(half - 1), :] = low[ch]
            work[ch, rows(half), :] = high[ch]
        for x in range(half - 2, -1, -1):
            far = length - 1 - x
            for ch in chains:
                scale = factor(ch, x)
                low[ch] = work[ch, rows(x), :] + scale * low[ch]
                high[ch] = work[ch, rows(far), :] + scale * high[ch]
                work[ch, rows(x), :] = low[ch]
                work[ch, rows(far), :] = high[ch]

    def half_step(work, other, before, after):
        share = BLOCK // 4
        for cls in range(4):
            result = begin(work, cls, fwd_ref)
            for t in range(cls * share, (cls + 1) * share):
                gather(other, before * BLOCK + t, t)
            if cls == 2:
                sweep(work, range(4))
            finish(work, cls, result)
        for cls in range(4):
            result = begin(work, cls, bwd_ref)
            if cls == 0:
                sweep(work, range(4, 8))
            for t in range(cls * share, (cls + 1) * share):
                multiply(other, after * BLOCK + t, t)
            finish(work, cls, result)

    for t in range(BLOCK):
        multiply(even_work, t, t)
    for table in tables[1:]:
        table.wait()

    def run_pair(step, carry):
        half_step(even_work, odd_work, 2 * step - 1, 2 * step + 1)
        half_step(odd_work, even_work, 2 * step, 2 * step + 2)
        return carry

    pairs = (live_count + 2 * BLOCK - 1) // (2 * BLOCK)
    lax.fori_loop(0, pairs, run_pair, 0)
    for t in range(BLOCK):
        gather(odd_work, (2 * pairs - 1) * BLOCK + t, t)

    def send_out(owner, carry):
        top = jnp.abs(totals[owner * 8])
        for k in range(1, 8):
            top = jnp.maximum(top, jnp.abs(totals[owner * 8 + k]))
        top = jnp.maximum(jnp.max(top, axis=0, keepdims=True), 2.0**-110)
        power = jnp.ceil(jnp.log2(top) + 1e-4)
        gain = jnp.exp2(-power) * LEVELS
        for k in range(8):
            level = jnp.round(totals[owner * 8 + k] * gain).astype(jnp.int32).astype(jnp.int16)
            for lh in range(2):
                first = (k * 2 + lh) * half
                out_ref[owner, first : first + half, :] = level[:, lh * 128 : (lh + 1) * 128]
        codes = jnp.concatenate(
            [jnp.broadcast_to(power[:, lh * 128 : (lh + 1) * 128], (8, 128)) for lh in range(2)], axis=0
        )
        out_ref[owner, 16 * half :, :] = codes.astype(jnp.int32).astype(jnp.int16)
        departure(owner).start()
        return carry

    def departure(owner):
        return pltpu.make_async_copy(out_ref.at[owner], out_hbm.at[owner], out_sems.at[owner])

    def leave(owner, carry):
        departure(owner).wait()
        return carry

    lax.fori_loop(0, nodes, send_out, 0)
    lax.fori_loop(0, nodes, leave, 0)


def final_kernel(asked_ref, in_ref, code_ref, table_ref, out_ref, totals, work):
    nodes = in_ref.shape[0]
    orbs, width = out_ref.shape
    half = totals.shape[1] // orbs
    plane = width // half
    pitch = half + 1
    totals[...] = jnp.zeros_like(totals)

    def add_one(node, carry):
        target = asked_ref[node, 0, 0]

        @pl.when(target >= 0)
        def _():
            codes = code_ref[node].astype(jnp.int32).astype(F32)
            start = pl.multiple_of(target * half, half)
            for lh in range(2):
                gain = jnp.exp2(codes[lh * 8 : lh * 8 + 1]) * (1.0 / LEVELS)
                for pos in range(4):
                    first = (pos * 2 + lh) * half
                    level = in_ref[node, first : first + half, :].astype(jnp.int32).astype(F32)
                    totals[pos * 2 + lh, pl.ds(start, half), :] += level * gain

        return carry

    lax.fori_loop(0, nodes, add_one, 0)
    for py in range(2):
        rows = jnp.concatenate([totals[py * 4 + j] for j in range(4)], axis=1)
        high, low = halves(rows)
        result = jnp.dot(high, table_ref[py], preferred_element_type=F32) + jnp.dot(
            low, table_ref[py], preferred_element_type=F32
        )
        for j in range(4):
            for orb in range(orbs):
                work[py * 4 + j, orb * pitch : orb * pitch + half, :] = result[
                    orb * half : (orb + 1) * half, j * 128 : (j + 1) * 128
                ]
    for x in range(half):
        for j in range(plane // 128):
            out_ref[:, x * plane + j * 128 : x * plane + (j + 1) * 128] = work[
                j, pl.ds(x, orbs, stride=pitch), :
            ]


def call_solve(orbs, fetch, offsets, pairs, count, incoming):
    nodes, length, plane = incoming.shape
    half = length // 2
    area = half * half
    tables = host_tables(length)
    smem = pl.BlockSpec(memory_space=pltpu.SMEM)
    hbm = pl.BlockSpec(memory_space=pl.ANY)
    work = pltpu.VMEM((8, length * PITCH, 128), F32)
    steps = (pairs.shape[0] // 2 + 2 * BLOCK - 1) // (2 * BLOCK)
    return pl.pallas_call(
        functools.partial(solve_kernel, orbs),
        out_shape=jax.ShapeDtypeStruct((nodes, 16 * half + 16, 128), jnp.int16),
        in_specs=[smem] * 4 + [hbm] * 5,
        out_specs=hbm,
        scratch_shapes=[
            pltpu.VMEM((nodes * 32 + 1, half, area), BF16),
            work,
            work,
            pltpu.VMEM((nodes * 8, half, area), F32),
            pltpu.SMEM(((2 * steps + 2) * BLOCK * 9,), jnp.int32),
            pltpu.VMEM((4, 3 * area, area), BF16),
            pltpu.VMEM((4, 3 * area, area), BF16),
            pltpu.VMEM((8, half + 8, 128), F32),
            pltpu.VMEM((area, 3 * area), BF16),
            pltpu.VMEM((nodes, length, plane), BF16),
            pltpu.VMEM((nodes, 16 * half + 16, 128), jnp.int16),
            pltpu.SemaphoreType.DMA((4,)),
            pltpu.SemaphoreType.DMA((nodes // 8,)),
            pltpu.SemaphoreType.DMA((nodes,)),
        ],
        compiler_params=pltpu.CompilerParams(vmem_limit_bytes=56 << 20),
        name="solve",
    )(
        fetch, offsets, pairs, count, incoming,
        tables["variants"], tables["forward"], tables["backward"], tables["factors"],
    )


def on_device(phi, offsets, fetch, task_pairs, task_count):
    nodes = lax.axis_size("orb")
    orbs, volume = phi.shape
    length = cube_root(volume)
    half, plane = length // 2, length * length
    tables = host_tables(length)
    smem = pl.BlockSpec(memory_space=pltpu.SMEM)
    vmem = pl.BlockSpec(memory_space=pltpu.VMEM)
    hbm = pl.BlockSpec(memory_space=pl.ANY)
    params = pltpu.CompilerParams(vmem_limit_bytes=56 << 20)
    fetch = fetch.reshape(-1)
    asking = pl.pallas_call(
        ask_kernel,
        out_shape=jax.ShapeDtypeStruct((nodes, 1, 128), jnp.int32),
        in_specs=[smem],
        out_specs=vmem,
        name="ask",
    )(fetch)
    packed = pl.pallas_call(
        pack_kernel,
        out_shape=jax.ShapeDtypeStruct((orbs, length, plane), BF16),
        in_specs=[vmem, vmem],
        out_specs=vmem,
        scratch_shapes=[pltpu.VMEM((plane // 128, (orbs + 1) * length, 128), F32)],
        compiler_params=params,
        name="pack",
    )(phi, tables["pack"])
    asked = lax.all_to_all(asking, "orb", split_axis=0, concat_axis=0, tiled=True)
    outgoing = pl.pallas_call(
        pick_kernel,
        out_shape=jax.ShapeDtypeStruct((nodes, length, plane), BF16),
        in_specs=[smem, hbm],
        out_specs=hbm,
        scratch_shapes=[pltpu.SemaphoreType.DMA((nodes,))],
        name="pick",
    )(asked, packed)
    incoming = lax.all_to_all(outgoing, "orb", split_axis=0, concat_axis=0, tiled=True)
    partial = call_solve(
        orbs, fetch, offsets.reshape(-1), task_pairs.reshape(-1), task_count, incoming
    )
    returned = lax.all_to_all(partial, "orb", split_axis=0, concat_axis=0, tiled=True)
    return pl.pallas_call(
        final_kernel,
        grid=(2,),
        out_shape=jax.ShapeDtypeStruct((orbs, volume), F32),
        in_specs=[
            smem,
            pl.BlockSpec((nodes, 8 * half, 128), lambda hx: (0, hx, 0)),
            pl.BlockSpec((nodes, 16, 128), lambda hx: (0, half, 0)),
            pl.BlockSpec((2, plane // 2, plane // 2), lambda hx: (0, 0, 0)),
        ],
        out_specs=pl.BlockSpec((orbs, volume // 2), lambda hx: (0, hx)),
        scratch_shapes=[
            pltpu.VMEM((8, orbs * half, 128), F32),
            pltpu.VMEM((plane // 128, orbs * (half + 1), 128), F32),
        ],
        compiler_params=params,
        name="final",
    )(asked, returned, returned, tables["unpack"])


def solution(mesh):
    in_specs = (
        P(("groups", "orb"), None),
        P("groups", None),
        P(("groups", "orb"), None),
        P(("groups", "orb"), None),
        P(("groups", "orb")),
    )
    out_specs = P(("groups", "orb"), None)
    return jax.shard_map(
        on_device, mesh=mesh, in_specs=in_specs, out_specs=out_specs, check_vma=False
    )
```

time: 106 us -> 133 us (1.25)
  Pallas kernels: 27.8 us -> 58.5 us
  local copies, waits for them, and re-layouts: 5.87 us -> 3.25 us
  other arithmetic: 1.81 us -> 0 us
    pallas_call x2 -> x4, Pallas kernels: 24.1 us -> 55.4 us  [the longest x1 33.8 us: on_device(): pl.pallas_call(pick_kernel, out_shape=jax.ShapeDtypeStruct((nodes, length...]
    gather x1 -> x0, local copies, waits for them, and re-layouts: 1.84 us -> none  [on_device(): outgoing = jnp.take(packed, jnp.maximum(wanted, 0), axis=0)]
  transfers between devices with their start and end apart: 2 -> 2, of which waited for: 2 -> 2; matrix products, arithmetic and copies ran while one was open for 2% -> 1% of each run, Pallas kernels for 3% -> 2%
where the time goes in v2:
time: 133 us; the launch traced here: 132 us
  Pallas kernels  58.5 us (44%)
  blocking collectives  35.1 us (26%)
  waiting for transfers between devices  23.8 us (18%)
  starting transfers between devices  11.1 us (8%)
  local copies, waits for them, and re-layouts  3.25 us (2%)
    all_to_all x1, blocking collectives, on_device(): lax.all_to_all(partial, 'orb', split_axis=0, concat_axis=0, tiled=True)  35.1 us
    pallas_call x1, Pallas kernels, on_device(): pl.pallas_call(pick_kernel, out_shape=jax.ShapeDtypeStruct((nodes, length...  33.8 us
    all_to_all x1, waiting for transfers between devices, on_device(): lax.all_to_all(outgoing, 'orb', split_axis=0, concat_axis=0, tiled=True)  20.5 us
    pallas_call x1, Pallas kernels, call_solve(): pl.pallas_call(functools.partial(solve_kernel, orbs), out_shape=jax.Shape...  15.4 us
    all_to_all x1, starting transfers between devices, on_device(): lax.all_to_all(asking, 'orb', split_axis=0, concat_axis=0, tiled=True)  7.39 us
    pallas_call x1, Pallas kernels, on_device(): pl.pallas_call(final_kernel, grid=(2,), out_shape=jax.ShapeDtypeStruct((o...  4.92 us
    all_to_all x1, starting transfers between devices, on_device(): lax.all_to_all(outgoing, 'orb', split_axis=0, concat_axis=0, tiled=True)  3.66 us
    all_to_all x1, waiting for transfers between devices, on_device(): lax.all_to_all(asking, 'orb', split_axis=0, concat_axis=0, tiled=True)  3.23 us
  transfers between devices with their start and end apart: 2, of which 2 were waited for; matrix products, arithmetic and copies ran while one was open for 1% of the time, Pallas kernels for 2%

profile of v2, /device:TPU:0, one launch (start us, length us, event | category | flops | bytes accessed | tf_op | source)
XLA Modules:
  0.0 132.4 jit_solution(13309920998549609825)
XLA Ops:
  0.0 1.3 ask.1
  1.3 7.4 %all-to-all-start = ((s32[16,1,128]{2,1,0:T(1,128)}), s32[16,1,128]{2,1,0:T(1,128)S(1)}, u32[]{:S(2)}, u32[]{:S(2)}) async-start(s32[16,1,128]{2,1,0:T(1,128)} %ask.1), calls=%async_computation | async-start | bytes 16384 | tf_op jit(solution)/shard_map/all_to_all | solution.py:463
  8.7 3.2 %pack.1.packed_ref = bf16[16,32,1024]{2,1,0:T(8,128)(2,1)} custom-call(bf16[16,32768]{1,0:T(8,128)(2,1)} %phi_ref.1, bf16[512,512]{1,0:T(8,128)(2,1)} %constant.12.clone.table_ref), custom_call_target="tpu_custom_call" | custom-call | tf_op jit(solution)/shard_map/pack/pallas_call | solution.py:454
  11.8 3.2 %all-to-all-done.asked_ref = s32[16,1,128]{2,1,0:T(1,128)S(1)} async-done(((s32[16,1,128]{2,1,0:T(1,128)}), s32[16,1,128]{2,1,0:T(1,128)S(1)}, u32[]{:S(2)}, u32[]{:S(2)}) %all-to-all-start) | async-done | bytes 8224 | tf_op jit(solution)/shard_map/all_to_all | solution.py:463
  15.1 0.0 copy-start.1
  15.1 0.6 copy-done.1
  15.7 33.8 %pick.1 = bf16[16,32,1024]{2,1,0:T(8,128)(2,1)} custom-call(s32[16,1,128]{2,1,0:T(1,128)} %copy-done.1, bf16[16,32,1024]{2,1,0:T(8,128)(2,1)} %pack.1.packed_ref), custom_call_target="tpu_custom_call" | custom-call | tf_op jit(solution)/shard_map/pick/pallas_call | solution.py:464
  49.5 0.0 copy-start.3
  49.5 0.0 copy-start.2
  49.5 3.7 %all-to-all-start.1 = ((bf16[16,32,1024]{2,1,0:T(8,128)(2,1)}), bf16[16,32,1024]{2,1,0:T(8,128)(2,1)S(1)}, u32[]{:S(2)}, u32[]{:S(2)}) async-start(bf16[16,32,1024]{2,1,0:T(8,128)(2,1)} %pick.1), calls=%async_computation.1 | async-start | bytes 2097152 | tf_op jit(solution)/shard_map/all_to_all | solution.py:472
  53.8 0.0 copy-done.3
  53.8 0.1 copy.14
  53.9 0.7 reshape.11.pairs_ref
  54.6 0.0 copy-done.2
  54.6 0.1 copy.13
  54.7 0.8 reshape.10.offsets_ref
  55.5 20.5 %all-to-all-done.1.in_hbm = bf16[16,32,1024]{2,1,0:T(8,128)(2,1)S(1)} async-done(((bf16[16,32,1024]{2,1,0:T(8,128)(2,1)}), bf16[16,32,1024]{2,1,0:T(8,128)(2,1)S(1)}, u32[]{:S(2)}, u32[]{:S(2)}) %all-to-all-start.1) | async-done | bytes 1048608 | tf_op jit(solution)/shard_map/all_to_all | solution.py:472
  76.1 0.0 copy-start
  76.1 1.0 copy-done
  77.0 15.4 %solve.1 = s16[16,272,128]{2,1,0:T(8,128)(2,1)} custom-call(s32[16]{0:T(128)} %bitcast.2, s32[768]{0:T(1024)} %reshape.10.offsets_ref, s32[96]{0:T(128)} %reshape.11.pairs_ref, s32[1]{0:T(128)S(6)} %copy.15.count_ref, bf16[16,32,1024]{2,1,0:T(8,128)(2,1)} %copy-done, bf16[256,768]{1,0:T(8,128)(2,1)} %constant.13.clone.var_hbm, ...), custom_call_target="tpu_custom_call" | custom-call | tf_op jit(solution)/shard_map/solve/pallas_call | solution.py:407
  92.4 35.1 %all_to_all.15.in_ref.code_ref = s16[16,272,128]{2,1,0:T(8,128)(2,1)} all-to-all(s16[16,272,128]{2,1,0:T(8,128)(2,1)} %solve.1), channel_id=1, replica_groups=mesh['groups'=2,'orb'=16] {'orb'}, dimensions={0} | all-to-all | bytes 2228224 | tf_op jit(solution)/shard_map/all_to_all | solution.py:476
  127.5 4.9 %final.1 = f32[16,32768]{1,0:T(8,128)} custom-call(s32[16,1,128]{2,1,0:T(1,128)} %copy-done.1, s16[16,272,128]{2,1,0:T(8,128)(2,1)} %all_to_all.15.in_ref.code_ref, s16[16,272,128]{2,1,0:T(8,128)(2,1)} %all_to_all.15.in_ref.code_ref, bf16[2,512,512]{2,1,0:T(8,128)(2,1)} %constant.17.clone.table_ref), custom_call_target="tpu_custom_call" | custom-call | tf_op jit(solution)/shard_map/final/pallas_call | solution.py:477
Async XLA Ops:
  1.3 13.8 %all-to-all-start = ((s32[16,1,128]{2,1,0:T(1,128)}), s32[16,1,128]{2,1,0:T(1,128)S(1)}, u32[]{:S(2)}, u32[]{:S(2)}) async-start(s32[16,1,128]{2,1,0:T(1,128)} %ask.1), calls=%async_computation | async-start | bytes 16384 | tf_op jit(solution)/shard_map/all_to_all | solution.py:463
  15.1 0.6 copy-start.1
  49.5 4.3 %copy-start.3 = (s32[48,2]{0,1:T(2,128)S(1)}, s32[48,2]{0,1:T(2,128)}, u32[]{:S(2)}) copy-start(s32[48,2]{0,1:T(2,128)} %param.14) | copy-start | bytes 1156
  49.5 5.1 %copy-start.2 = (s32[256,3]{0,1:T(4,128)S(1)}, s32[256,3]{0,1:T(4,128)}, u32[]{:S(2)}) copy-start(s32[256,3]{0,1:T(4,128)} %param.12) | copy-start | bytes 9220
  49.5 26.6 %all-to-all-start.1 = ((bf16[16,32,1024]{2,1,0:T(8,128)(2,1)}), bf16[16,32,1024]{2,1,0:T(8,128)(2,1)S(1)}, u32[]{:S(2)}, u32[]{:S(2)}) async-start(bf16[16,32,1024]{2,1,0:T(8,128)(2,1)} %pick.1), calls=%async_computation.1 | async-start | bytes 2097152 | tf_op jit(solution)/shard_map/all_to_all | solution.py:472
  76.1 1.0 copy-start

commit v3 on v2

--- a/solution.py
+++ b/solution.py
@@ -118,46 +118,31 @@
             out_ref[orb, :, j * 128 : (j + 1) * 128] = piece.astype(BF16)
 
 
-def pick_kernel(asked_ref, packed_ref, out_ref, sems):
-    nodes = out_ref.shape[0]
-    copies = []
-    for node in range(nodes):
-        orb = jnp.maximum(asked_ref[node, 0, 0], 0)
-        copies.append(pltpu.make_async_copy(packed_ref.at[orb], out_ref.at[node], sems.at[node]))
-        copies[-1].start()
-    for copy in copies:
-        copy.wait()
+def pick_kernel(asked_ref, packed_ref, out_ref):
+    for node in range(out_ref.shape[0]):
+        out_ref[node] = packed_ref[jnp.maximum(asked_ref[node, 0, 0], 0)]
 
 
 def solve_kernel(
-    orbs, fetch_ref, offsets_ref, pairs_ref, count_ref, in_hbm, var_hbm, fwd_hbm, bwd_hbm, fac_hbm,
-    out_hbm, octs, even_work, odd_work, totals, plan, fwd_ref, bwd_ref, fac_ref, var_ref, in_ref,
-    out_ref, sems, in_sems, out_sems,
+    orbs, fetch_ref, offsets_ref, pairs_ref, count_ref, in_ref, var_ref, fwd_hbm, bwd_hbm, fac_hbm,
+    out_ref, octs, even_work, odd_work, totals, plan, fwd_ref, bwd_ref, fac_ref, sems,
 ):
     nodes, length = in_ref.shape[0], in_ref.shape[1]
     half = length // 2
     area = half * half
     zero_at = nodes * 32
     group = 8
-    sources = ((var_hbm, var_ref), (fwd_hbm, fwd_ref), (bwd_hbm, bwd_ref), (fac_hbm, fac_ref))
+    sources = ((fwd_hbm, fwd_ref), (bwd_hbm, bwd_ref), (fac_hbm, fac_ref))
     tables = [
         pltpu.make_async_copy(source, target, sems.at[k]) for k, (source, target) in enumerate(sources)
     ]
-    def arrival(step):
-        spots = pl.ds(step * group, group)
-        return pltpu.make_async_copy(in_hbm.at[spots], in_ref.at[spots], in_sems.at[step])
-
-    tables[0].start()
-    for step in range(nodes // group):
-        arrival(step).start()
-    for table in tables[1:]:
+    for table in tables:
         table.start()
     octs[zero_at] = jnp.zeros((half, area), BF16)
     live_count = count_ref[0]
     last_slot = pairs_ref.shape[0] // 2 - 1
 
     def make_variants(step, carry):
-        arrival(step).wait()
         for quad in range(4):
             block = in_ref[pl.ds(step * group, group), :, quad * area : (quad + 1) * area]
             turned = jnp.dot(
@@ -172,7 +157,6 @@
                         octs[base + 1 + rev] = turned[first : first + half, rev * area : (rev + 1) * area]
         return carry
 
-    tables[0].wait()
     lax.fori_loop(0, nodes // group, make_variants, 0)
 
     def clear(step, carry):
@@ -309,7 +293,7 @@
 
     for t in range(BLOCK):
         multiply(even_work, t, t)
-    for table in tables[1:]:
+    for table in tables:
         table.wait()
 
     def run_pair(step, carry):
@@ -338,18 +322,9 @@
             [jnp.broadcast_to(power[:, lh * 128 : (lh + 1) * 128], (8, 128)) for lh in range(2)], axis=0
         )
         out_ref[owner, 16 * half :, :] = codes.astype(jnp.int32).astype(jnp.int16)
-        departure(owner).start()
         return carry
 
-    def departure(owner):
-        return pltpu.make_async_copy(out_ref.at[owner], out_hbm.at[owner], out_sems.at[owner])
-
-    def leave(owner, carry):
-        departure(owner).wait()
-        return carry
-
     lax.fori_loop(0, nodes, send_out, 0)
-    lax.fori_loop(0, nodes, leave, 0)
 
 
 def final_kernel(asked_ref, in_ref, code_ref, table_ref, out_ref, totals, work):
@@ -407,8 +382,8 @@
     return pl.pallas_call(
         functools.partial(solve_kernel, orbs),
         out_shape=jax.ShapeDtypeStruct((nodes, 16 * half + 16, 128), jnp.int16),
-        in_specs=[smem] * 4 + [hbm] * 5,
-        out_specs=hbm,
+        in_specs=[smem] * 4 + [pl.BlockSpec(memory_space=pltpu.VMEM)] * 2 + [hbm] * 3,
+        out_specs=pl.BlockSpec(memory_space=pltpu.VMEM),
         scratch_shapes=[
             pltpu.VMEM((nodes * 32 + 1, half, area), BF16),
             work,
@@ -418,14 +393,9 @@
             pltpu.VMEM((4, 3 * area, area), BF16),
             pltpu.VMEM((4, 3 * area, area), BF16),
             pltpu.VMEM((8, half + 8, 128), F32),
-            pltpu.VMEM((area, 3 * area), BF16),
-            pltpu.VMEM((nodes, length, plane), BF16),
-            pltpu.VMEM((nodes, 16 * half + 16, 128), jnp.int16),
-            pltpu.SemaphoreType.DMA((4,)),
-            pltpu.SemaphoreType.DMA((nodes // 8,)),
-            pltpu.SemaphoreType.DMA((nodes,)),
+            pltpu.SemaphoreType.DMA((3,)),
         ],
-        compiler_params=pltpu.CompilerParams(vmem_limit_bytes=56 << 20),
+        compiler_params=pltpu.CompilerParams(vmem_limit_bytes=(10 << 20) + nodes * (704 << 10)),
         name="solve",
     )(
         fetch, offsets, pairs, count, incoming,
@@ -441,8 +411,7 @@
     tables = host_tables(length)
     smem = pl.BlockSpec(memory_space=pltpu.SMEM)
     vmem = pl.BlockSpec(memory_space=pltpu.VMEM)
-    hbm = pl.BlockSpec(memory_space=pl.ANY)
-    params = pltpu.CompilerParams(vmem_limit_bytes=56 << 20)
+    params = pltpu.CompilerParams(vmem_limit_bytes=(12 << 20) + nodes * (384 << 10))
     fetch = fetch.reshape(-1)
     asking = pl.pallas_call(
         ask_kernel,
@@ -464,9 +433,9 @@
     outgoing = pl.pallas_call(
         pick_kernel,
         out_shape=jax.ShapeDtypeStruct((nodes, length, plane), BF16),
-        in_specs=[smem, hbm],
-        out_specs=hbm,
-        scratch_shapes=[pltpu.SemaphoreType.DMA((nodes,))],
+        in_specs=[smem, vmem],
+        out_specs=vmem,
+        compiler_params=params,
         name="pick",
     )(asked, packed)
     incoming = lax.all_to_all(outgoing, "orb", split_axis=0, concat_axis=0, tiled=True)

time: 133 us -> 97.1 us (0.73)
  Pallas kernels: 58.5 us -> 21.1 us
    pallas_call x1, Pallas kernels: 33.8 us -> 1.71 us  [on_device(): pl.pallas_call(pick_kernel, out_shape=jax.ShapeDtypeStruct((nodes, length...]
    pallas_call x1, Pallas kernels: 3.16 us -> 0.83 us  [on_device(): pl.pallas_call(pack_kernel, out_shape=jax.ShapeDtypeStruct((orbs, length,...]
    pallas_call x1, Pallas kernels: 15.4 us -> 13.1 us  [call_solve(): pl.pallas_call(functools.partial(solve_kernel, orbs), out_shape=jax.Shape...]
    unnamed x10 -> x22, local copies, waits for them, and re-layouts: 1.8 us -> 3.92 us
  transfers between devices with their start and end apart: 2 -> 2, of which waited for: 2 -> 2; matrix products, arithmetic and copies ran while one was open for 1% -> 1% of each run, Pallas kernels for 2% -> 1%
where the time goes in v3:
time: 97.1 us
  blocking collectives  34.9 us (36%)
  waiting for transfers between devices  24.9 us (26%)
  Pallas kernels  21.1 us (22%)
  starting transfers between devices  11.2 us (12%)
  local copies, waits for them, and re-layouts  4.25 us (4%)
    all_to_all x1, blocking collectives, on_device(): lax.all_to_all(partial, 'orb', split_axis=0, concat_axis=0, tiled=True)  34.9 us
    all_to_all x1, waiting for transfers between devices, on_device(): lax.all_to_all(outgoing, 'orb', split_axis=0, concat_axis=0, tiled=True)  21.7 us
    pallas_call x1, Pallas kernels, call_solve(): pl.pallas_call(functools.partial(solve_kernel, orbs), out_shape=jax.Shape...  13.1 us
    all_to_all x1, starting transfers between devices, on_device(): lax.all_to_all(asking, 'orb', split_axis=0, concat_axis=0, tiled=True)  7.39 us
    pallas_call x1, Pallas kernels, on_device(): pl.pallas_call(final_kernel, grid=(2,), out_shape=jax.ShapeDtypeStruct((o...  4.25 us
    unnamed x22, local copies, waits for them, and re-layouts  3.92 us
    all_to_all x1, starting transfers between devices, on_device(): lax.all_to_all(outgoing, 'orb', split_axis=0, concat_axis=0, tiled=True)  3.8 us
    all_to_all x1, waiting for transfers between devices, on_device(): lax.all_to_all(asking, 'orb', split_axis=0, concat_axis=0, tiled=True)  3.22 us
  transfers between devices with their start and end apart: 2, of which 2 were waited for; matrix products, arithmetic and copies ran while one was open for 1% of the time, Pallas kernels for 1%

profile of v3, /device:TPU:0, one launch (start us, length us, event | category | flops | bytes accessed | tf_op | source)
XLA Modules:
  0.0 97.1 jit_solution(759837788396683973)
XLA Ops:
  0.0 1.3 %ask.1 = s32[16,1,128]{2,1,0:T(1,128)} custom-call(s32[16]{0:T(128)} %bitcast.1), custom_call_target="tpu_custom_call" | custom-call | tf_op jit(solution)/shard_map/ask/pallas_call | solution.py:416
  1.3 7.4 %all-to-all-start = ((s32[16,1,128]{2,1,0:T(1,128)}), s32[16,1,128]{2,1,0:T(1,128)S(1)}, u32[]{:S(2)}, u32[]{:S(2)}) async-start(s32[16,1,128]{2,1,0:T(1,128)} %ask.1), calls=%async_computation | async-start | bytes 16384 | tf_op jit(solution)/shard_map/all_to_all | solution.py:432
  8.7 0.0 copy-start.2
  8.7 1.2 %copy-done.2 = bf16[16,32768]{1,0:T(8,128)(2,1)S(1)} copy-done((bf16[16,32768]{1,0:T(8,128)(2,1)S(1)}, bf16[16,32768]{1,0:T(8,128)(2,1)}, u32[]{:S(2)}) %copy-start.2) | copy-done | bytes 1048600
  9.9 0.0 copy-start.4
  9.9 1.0 %copy-done.4 = bf16[512,512]{1,0:T(8,128)(2,1)S(1)} copy-done((bf16[512,512]{1,0:T(8,128)(2,1)S(1)}, bf16[512,512]{1,0:T(8,128)(2,1)}, u32[]{:S(2)}) %copy-start.4) | copy-done | bytes 524312
  10.9 0.8 pack.1.packed_ref
  11.8 3.2 %all-to-all-done.asked_ref = s32[16,1,128]{2,1,0:T(1,128)S(1)} async-done(((s32[16,1,128]{2,1,0:T(1,128)}), s32[16,1,128]{2,1,0:T(1,128)S(1)}, u32[]{:S(2)}, u32[]{:S(2)}) %all-to-all-start) | async-done | bytes 8224 | tf_op jit(solution)/shard_map/all_to_all | solution.py:432
  15.0 1.7 %pick.1 = bf16[16,32,1024]{2,1,0:T(8,128)(2,1)} custom-call(s32[16,1,128]{2,1,0:T(1,128)S(1)} %all-to-all-done.asked_ref, bf16[16,32,1024]{2,1,0:T(8,128)(2,1)S(1)} %pack.1.packed_ref), custom_call_target="tpu_custom_call" | custom-call | tf_op jit(solution)/shard_map/pick/pallas_call | solution.py:433
  16.7 0.0 copy-start.9
  16.7 0.0 copy-start.8
  16.7 0.0 copy-start
  16.7 0.0 copy-start.5
  16.7 0.0 copy-start.6
  16.7 0.0 copy-start.7
  16.7 3.8 %all-to-all-start.1 = ((bf16[16,32,1024]{2,1,0:T(8,128)(2,1)}), bf16[16,32,1024]{2,1,0:T(8,128)(2,1)S(1)}, u32[]{:S(2)}, u32[]{:S(2)}) async-start(bf16[16,32,1024]{2,1,0:T(8,128)(2,1)} %pick.1), calls=%async_computation.1 | async-start | bytes 2097152 | tf_op jit(solution)/shard_map/all_to_all | solution.py:441
  21.2 0.0 copy-done.9
  21.2 0.1 copy.14
  21.3 0.1 reshape.11.pairs_ref
  21.4 0.0 copy-done.8
  21.4 0.1 copy.13
  21.6 0.2 reshape.10.offsets_ref
  21.8 21.7 %all-to-all-done.1.in_ref = bf16[16,32,1024]{2,1,0:T(8,128)(2,1)S(1)} async-done(((bf16[16,32,1024]{2,1,0:T(8,128)(2,1)}), bf16[16,32,1024]{2,1,0:T(8,128)(2,1)S(1)}, u32[]{:S(2)}, u32[]{:S(2)}) %all-to-all-start.1) | async-done | bytes 1048608 | tf_op jit(solution)/shard_map/all_to_all | solution.py:441
  43.4 0.0 copy-done
  43.4 0.0 copy-done.5
  43.4 0.0 copy-done.6
  43.5 0.0 copy-done.7
  43.5 0.0 copy-start.1
  43.5 1.4 %copy-done.1 = bf16[4,768,256]{2,1,0:T(8,128)(2,1)S(1)} copy-done((bf16[4,768,256]{2,1,0:T(8,128)(2,1)S(1)}, bf16[4,768,256]{2,1,0:T(8,128)(2,1)}, u32[]{:S(2)}) %copy-start.1) | copy-done | bytes 1572888
  44.9 13.1 %solve.1 = s16[16,272,128]{2,1,0:T(8,128)(2,1)S(1)} custom-call(s32[16]{0:T(128)S(1)} %bitcast.2, s32[768]{0:T(1024)S(1)} %reshape.10.offsets_ref, s32[96]{0:T(128)S(1)} %reshape.11.pairs_ref, s32[1]{0:T(128)S(6)} %copy.15.count_ref, bf16[16,32,1024]{2,1,0:T(8,128)(2,1)S(1)} %all-to-all-done.1.in_ref, bf16[256,768]{1,0:T(8,128)(2,1)S(1)} %copy-done.5, ...), custom_call_target="tpu_custom_call" | custom-call | tf_op jit(solution)/shard_map/solve/pallas_call | solution.py:382
  58.0 0.0 copy-start.3
  58.0 34.9 %all_to_all.15.in_ref.code_ref = s16[16,272,128]{2,1,0:T(8,128)(2,1)S(1)} all-to-all(s16[16,272,128]{2,1,0:T(8,128)(2,1)S(1)} %solve.1), channel_id=1, replica_groups=mesh['groups'=2,'orb'=16] {'orb'}, dimensions={0} | all-to-all | bytes 2228224 | tf_op jit(solution)/shard_map/all_to_all | solution.py:445
  92.9 0.0 copy-done.3
  92.9 4.2 %final.1 = f32[16,32768]{1,0:T(8,128)} custom-call(s32[16,1,128]{2,1,0:T(1,128)S(1)} %all-to-all-done.asked_ref, s16[16,272,128]{2,1,0:T(8,128)(2,1)S(1)} %all_to_all.15.in_ref.code_ref, s16[16,272,128]{2,1,0:T(8,128)(2,1)S(1)} %all_to_all.15.in_ref.code_ref, bf16[2,512,512]{2,1,0:T(8,128)(2,1)S(1)} %copy-done.3), custom_call_target="tpu_custom_call" | custom-call | tf_op jit(solution)/shard_map/final/pallas_call | solution.py:446
Async XLA Ops:
  1.3 13.7 %all-to-all-start = ((s32[16,1,128]{2,1,0:T(1,128)}), s32[16,1,128]{2,1,0:T(1,128)S(1)}, u32[]{:S(2)}, u32[]{:S(2)}) async-start(s32[16,1,128]{2,1,0:T(1,128)} %ask.1), calls=%async_computation | async-start | bytes 16384 | tf_op jit(solution)/shard_map/all_to_all | solution.py:432
  8.7 1.2 %copy-start.2 = (bf16[16,32768]{1,0:T(8,128)(2,1)S(1)}, bf16[16,32768]{1,0:T(8,128)(2,1)}, u32[]{:S(2)}) copy-start(bf16[16,32768]{1,0:T(8,128)(2,1)} %phi_ref.1) | copy-start | bytes 3145732
  9.9 1.0 %copy-start.4 = (bf16[512,512]{1,0:T(8,128)(2,1)S(1)}, bf16[512,512]{1,0:T(8,128)(2,1)}, u32[]{:S(2)}) copy-start(bf16[512,512]{1,0:T(8,128)(2,1)} %constant.12.clone.table_ref) | copy-start | bytes 1572868
  16.7 4.5 %copy-start.9 = (s32[48,2]{0,1:T(2,128)S(1)}, s32[48,2]{0,1:T(2,128)}, u32[]{:S(2)}) copy-start(s32[48,2]{0,1:T(2,128)} %param.14) | copy-start | bytes 1156
  16.7 4.7 %copy-start.8 = (s32[256,3]{0,1:T(4,128)S(1)}, s32[256,3]{0,1:T(4,128)}, u32[]{:S(2)}) copy-start(s32[256,3]{0,1:T(4,128)} %param.12) | copy-start | bytes 9220
  16.7 26.7 %copy-start = (bf16[4,768,256]{2,1,0:T(8,128)(2,1)S(1)}, bf16[4,768,256]{2,1,0:T(8,128)(2,1)}, u32[]{:S(2)}) copy-start(bf16[4,768,256]{2,1,0:T(8,128)(2,1)} %constant.15.clone.bwd_hbm) | copy-start | bytes 4718596
  16.7 26.7 %copy-start.5 = (bf16[256,768]{1,0:T(8,128)(2,1)S(1)}, bf16[256,768]{1,0:T(8,128)(2,1)}, u32[]{:S(2)}) copy-start(bf16[256,768]{1,0:T(8,128)(2,1)} %constant.13.clone.var_ref) | copy-start | bytes 1179652
  16.7 26.7 %copy-start.6 = (f32[8,24,128]{2,1,0:T(8,128)S(1)}, f32[8,24,128]{2,1,0:T(8,128)}, u32[]{:S(2)}) copy-start(f32[8,24,128]{2,1,0:T(8,128)} %constant.16.clone.fac_hbm) | copy-start | bytes 294916
  16.7 26.7 %copy-start.7 = (s32[1,16]{1,0:T(1,128)S(1)}, s32[1,16]{1,0:T(1,128)}, u32[]{:S(2)}) copy-start(s32[1,16]{1,0:T(1,128)} %param.13) | copy-start | bytes 196
  16.7 26.7 %all-to-all-start.1 = ((bf16[16,32,1024]{2,1,0:T(8,128)(2,1)}), bf16[16,32,1024]{2,1,0:T(8,128)(2,1)S(1)}, u32[]{:S(2)}, u32[]{:S(2)}) async-start(bf16[16,32,1024]{2,1,0:T(8,128)(2,1)} %pick.1), calls=%async_computation.1 | async-start | bytes 2097152 | tf_op jit(solution)/shard_map/all_to_all | solution.py:441
  43.5 1.4 %copy-start.1 = (bf16[4,768,256]{2,1,0:T(8,128)(2,1)S(1)}, bf16[4,768,256]{2,1,0:T(8,128)(2,1)}, u32[]{:S(2)}) copy-start(bf16[4,768,256]{2,1,0:T(8,128)(2,1)} %constant.14.clone.fwd_hbm) | copy-start | bytes 4718596
  58.0 34.9 %copy-start.3 = (bf16[2,512,512]{2,1,0:T(8,128)(2,1)S(1)}, bf16[2,512,512]{2,1,0:T(8,128)(2,1)}, u32[]{:S(2)}) copy-start(bf16[2,512,512]{2,1,0:T(8,128)(2,1)} %constant.17.clone.table_ref) | copy-start | bytes 3145732

commit v4 on v3

--- a/solution.py
+++ b/solution.py
@@ -41,9 +41,9 @@
         for par_z in (0, 1):
             table = np.kron(fold[par_y], fold[par_z])
             high, low = split_bf16(table)
-            forward.append(np.concatenate([high, high, low], axis=0))
+            forward.append(np.concatenate([high, low], axis=0))
             high, low = split_bf16(table.T)
-            backward.append(np.concatenate([high, high, low], axis=0))
+            backward.append(np.concatenate([high, low], axis=0))
             beta = 2.0 + (eigen[par_y::2][:, None] + eigen[par_z::2][None, :]).reshape(area)
             rows = [1.0 / beta]
             for _ in range(half - 1):
@@ -75,8 +75,7 @@
         one_hot[spot, y_nat * length + z_nat] = 1
         unpack.append(one_hot)
     return dict(
-        forward=np.stack(forward),
-        backward=np.stack(backward),
+        sines=np.stack([np.stack(forward), np.stack(backward)]),
         factors=np.stack(factors),
         variants=np.concatenate(variants, axis=1),
         pack=pack,
@@ -118,24 +117,32 @@
             out_ref[orb, :, j * 128 : (j + 1) * 128] = piece.astype(BF16)
 
 
-def pick_kernel(asked_ref, packed_ref, out_ref):
+def pick_kernel(asked_ref, packed_ref, out_ref, sems):
+    copies = []
     for node in range(out_ref.shape[0]):
-        out_ref[node] = packed_ref[jnp.maximum(asked_ref[node, 0, 0], 0)]
+        orb = jnp.maximum(asked_ref[node, 0, 0], 0)
+        copies.append(pltpu.make_async_copy(packed_ref.at[orb], out_ref.at[node], sems.at[node]))
+        copies[-1].start()
+    for copy in copies:
+        copy.wait()
 
 
 def solve_kernel(
-    orbs, fetch_ref, offsets_ref, pairs_ref, count_ref, in_ref, var_ref, fwd_hbm, bwd_hbm, fac_hbm,
-    out_ref, octs, even_work, odd_work, totals, plan, fwd_ref, bwd_ref, fac_ref, sems,
+    orbs, fetch_ref, offsets_ref, pairs_ref, count_ref, in_ref, var_ref, sine_hbm, fac_hbm,
+    out_ref, octs, even_work, odd_work, totals, plan, used, fwd_ref, bwd_ref, fac_ref, sems,
 ):
     nodes, length = in_ref.shape[0], in_ref.shape[1]
     half = length // 2
     area = half * half
     zero_at = nodes * 32
     group = 8
-    sources = ((fwd_hbm, fwd_ref), (bwd_hbm, bwd_ref), (fac_hbm, fac_ref))
-    tables = [
-        pltpu.make_async_copy(source, target, sems.at[k]) for k, (source, target) in enumerate(sources)
-    ]
+    area_rows = [pl.ds(0, area), pl.ds(area, area), pl.ds(2 * area, area)]
+    moves = [(fac_hbm, fac_ref)]
+    for way, target in enumerate((fwd_ref, bwd_ref)):
+        for part in range(3):
+            source = sine_hbm.at[way, :, area_rows[part // 2], :]
+            moves.append((source, target.at[:, area_rows[part], :]))
+    tables = [pltpu.make_async_copy(*move, sems.at[k]) for k, move in enumerate(moves)]
     for table in tables:
         table.start()
     octs[zero_at] = jnp.zeros((half, area), BF16)
@@ -162,6 +169,7 @@
     def clear(step, carry):
         for k in range(8):
             totals[step * 8 + k] = jnp.zeros((half, area), F32)
+        used[step] = 0
         return carry
 
     lax.fori_loop(0, nodes, clear, 0)
@@ -184,6 +192,7 @@
         live = slot < live_count
         note = (slot + BLOCK) * 9
         plan[note] = first
+        used[first] = jnp.where(live, 1, used[first])
         for hx in range(2):
             dens = []
             for pos in range(4):
@@ -307,21 +316,28 @@
         gather(odd_work, (2 * pairs - 1) * BLOCK + t, t)
 
     def send_out(owner, carry):
-        top = jnp.abs(totals[owner * 8])
-        for k in range(1, 8):
-            top = jnp.maximum(top, jnp.abs(totals[owner * 8 + k]))
-        top = jnp.maximum(jnp.max(top, axis=0, keepdims=True), 2.0**-110)
-        power = jnp.ceil(jnp.log2(top) + 1e-4)
-        gain = jnp.exp2(-power) * LEVELS
-        for k in range(8):
-            level = jnp.round(totals[owner * 8 + k] * gain).astype(jnp.int32).astype(jnp.int16)
-            for lh in range(2):
-                first = (k * 2 + lh) * half
-                out_ref[owner, first : first + half, :] = level[:, lh * 128 : (lh + 1) * 128]
-        codes = jnp.concatenate(
-            [jnp.broadcast_to(power[:, lh * 128 : (lh + 1) * 128], (8, 128)) for lh in range(2)], axis=0
-        )
-        out_ref[owner, 16 * half :, :] = codes.astype(jnp.int32).astype(jnp.int16)
+        @pl.when(used[owner] == 0)
+        def _():
+            out_ref[owner] = jnp.zeros(out_ref.shape[1:], jnp.int16)
+
+        @pl.when(used[owner] > 0)
+        def _():
+            top = jnp.abs(totals[owner * 8])
+            for k in range(1, 8):
+                top = jnp.maximum(top, jnp.abs(totals[owner * 8 + k]))
+            top = jnp.maximum(jnp.max(top, axis=0, keepdims=True), 2.0**-110)
+            power = jnp.ceil(jnp.log2(top) + 1e-4)
+            gain = jnp.exp2(-power) * LEVELS
+            for k in range(8):
+                level = jnp.round(totals[owner * 8 + k] * gain).astype(jnp.int32).astype(jnp.int16)
+                for lh in range(2):
+                    first = (k * 2 + lh) * half
+                    out_ref[owner, first : first + half, :] = level[:, lh * 128 : (lh + 1) * 128]
+            codes = jnp.concatenate(
+                [jnp.broadcast_to(power[:, lh * 128 : (lh + 1) * 128], (8, 128)) for lh in range(2)], axis=0
+            )
+            out_ref[owner, 16 * half :, :] = codes.astype(jnp.int32).astype(jnp.int16)
+
         return carry
 
     lax.fori_loop(0, nodes, send_out, 0)
@@ -382,7 +398,7 @@
     return pl.pallas_call(
         functools.partial(solve_kernel, orbs),
         out_shape=jax.ShapeDtypeStruct((nodes, 16 * half + 16, 128), jnp.int16),
-        in_specs=[smem] * 4 + [pl.BlockSpec(memory_space=pltpu.VMEM)] * 2 + [hbm] * 3,
+        in_specs=[smem] * 4 + [pl.BlockSpec(memory_space=pltpu.VMEM)] * 2 + [hbm] * 2,
         out_specs=pl.BlockSpec(memory_space=pltpu.VMEM),
         scratch_shapes=[
             pltpu.VMEM((nodes * 32 + 1, half, area), BF16),
@@ -390,16 +406,17 @@
             work,
             pltpu.VMEM((nodes * 8, half, area), F32),
             pltpu.SMEM(((2 * steps + 2) * BLOCK * 9,), jnp.int32),
+            pltpu.SMEM((nodes,), jnp.int32),
             pltpu.VMEM((4, 3 * area, area), BF16),
             pltpu.VMEM((4, 3 * area, area), BF16),
             pltpu.VMEM((8, half + 8, 128), F32),
-            pltpu.SemaphoreType.DMA((3,)),
+            pltpu.SemaphoreType.DMA((7,)),
         ],
         compiler_params=pltpu.CompilerParams(vmem_limit_bytes=(10 << 20) + nodes * (704 << 10)),
         name="solve",
     )(
         fetch, offsets, pairs, count, incoming,
-        tables["variants"], tables["forward"], tables["backward"], tables["factors"],
+        tables["variants"], tables["sines"], tables["factors"],
     )
 
 
@@ -434,7 +451,8 @@
         pick_kernel,
         out_shape=jax.ShapeDtypeStruct((nodes, length, plane), BF16),
         in_specs=[smem, vmem],
-        out_specs=vmem,
+        out_specs=pl.BlockSpec(memory_space=pl.ANY),
+        scratch_shapes=[pltpu.SemaphoreType.DMA((nodes,))],
         compiler_params=params,
         name="pick",
     )(asked, packed)

time: 97.1 us -> 98 us (level)
  local copies, waits for them, and re-layouts: 4.25 us -> 8.41 us
  waiting for transfers between devices: 24.9 us -> 20.8 us
    all_to_all x1, waiting for transfers between devices: 21.7 us -> 17.6 us  [on_device(): lax.all_to_all(outgoing, 'orb', split_axis=0, concat_axis=0, tiled=True)]
    unnamed x22 -> x20, local copies, waits for them, and re-layouts: 3.92 us -> 5.94 us
    reshape x1, local copies, waits for them, and re-layouts: 0.12 us -> 1.37 us  [on_device(): task_pairs.reshape(-1)]
  transfers between devices with their start and end apart: 2 -> 2, of which waited for: 2 -> 2; matrix products, arithmetic and copies ran while one was open for 1% -> 5% of each run, Pallas kernels for 1% -> 1%
where the time goes in v4:
time: 98 us; the launch traced here: 97.5 us
  blocking collectives  35.3 us (36%)
  Pallas kernels  21.2 us (22%)
  waiting for transfers between devices  20.8 us (21%)
  starting transfers between devices  11.1 us (11%)
  local copies, waits for them, and re-layouts  8.41 us (9%)
    all_to_all x1, blocking collectives, on_device(): lax.all_to_all(partial, 'orb', split_axis=0, concat_axis=0, tiled=True)  35.3 us
    all_to_all x1, waiting for transfers between devices, on_device(): lax.all_to_all(outgoing, 'orb', split_axis=0, concat_axis=0, tiled=True)  17.6 us
    pallas_call x1, Pallas kernels, call_solve(): pl.pallas_call(functools.partial(solve_kernel, orbs), out_shape=jax.Shape...  13.2 us
    all_to_all x1, starting transfers between devices, on_device(): lax.all_to_all(asking, 'orb', split_axis=0, concat_axis=0, tiled=True)  7.39 us
    unnamed x20, local copies, waits for them, and re-layouts  5.94 us
    pallas_call x1, Pallas kernels, on_device(): pl.pallas_call(final_kernel, grid=(2,), out_shape=jax.ShapeDtypeStruct((o...  4.14 us
    all_to_all x1, starting transfers between devices, on_device(): lax.all_to_all(outgoing, 'orb', split_axis=0, concat_axis=0, tiled=True)  3.67 us
    all_to_all x1, waiting for transfers between devices, on_device(): lax.all_to_all(asking, 'orb', split_axis=0, concat_axis=0, tiled=True)  3.17 us
  transfers between devices with their start and end apart: 2, of which 2 were waited for; matrix products, arithmetic and copies ran while one was open for 5% of the time, Pallas kernels for 1%

profile of v4, /device:TPU:0, one launch (start us, length us, event | category | flops | bytes accessed | tf_op | source)
XLA Modules:
  0.0 97.5 jit_solution(13020246595443880498)
XLA Ops:
  0.0 1.3 %ask.1 = s32[16,1,128]{2,1,0:T(1,128)} custom-call(s32[16]{0:T(128)} %bitcast.1), custom_call_target="tpu_custom_call" | custom-call | tf_op jit(solution)/shard_map/ask/pallas_call | solution.py:433
  1.3 7.4 %all-to-all-start = ((s32[16,1,128]{2,1,0:T(1,128)}), s32[16,1,128]{2,1,0:T(1,128)S(1)}, u32[]{:S(2)}, u32[]{:S(2)}) async-start(s32[16,1,128]{2,1,0:T(1,128)} %ask.1), calls=%async_computation | async-start | bytes 16384 | tf_op jit(solution)/shard_map/all_to_all | solution.py:449
  8.7 0.0 copy-start.1
  8.7 1.2 %copy-done.1 = bf16[16,32768]{1,0:T(8,128)(2,1)S(1)} copy-done((bf16[16,32768]{1,0:T(8,128)(2,1)S(1)}, bf16[16,32768]{1,0:T(8,128)(2,1)}, u32[]{:S(2)}) %copy-start.1) | copy-done | bytes 1048600
  9.9 0.0 copy-start.3
  9.9 1.0 %copy-done.3 = bf16[512,512]{1,0:T(8,128)(2,1)S(1)} copy-done((bf16[512,512]{1,0:T(8,128)(2,1)S(1)}, bf16[512,512]{1,0:T(8,128)(2,1)}, u32[]{:S(2)}) %copy-start.3) | copy-done | bytes 524312
  10.9 0.8 pack.1.packed_ref
  11.8 0.0 copy-start.8
  11.8 0.0 copy-start
  11.8 0.0 copy-start.4
  11.8 0.0 copy-start.6
  11.8 3.2 %all-to-all-done.asked_ref = s32[16,1,128]{2,1,0:T(1,128)S(1)} async-done(((s32[16,1,128]{2,1,0:T(1,128)}), s32[16,1,128]{2,1,0:T(1,128)S(1)}, u32[]{:S(2)}, u32[]{:S(2)}) %all-to-all-start) | async-done | bytes 8224 | tf_op jit(solution)/shard_map/all_to_all | solution.py:449
  15.0 1.8 %pick.1 = bf16[16,32,1024]{2,1,0:T(8,128)(2,1)} custom-call(s32[16,1,128]{2,1,0:T(1,128)S(1)} %all-to-all-done.asked_ref, bf16[16,32,1024]{2,1,0:T(8,128)(2,1)S(1)} %pack.1.packed_ref), custom_call_target="tpu_custom_call" | custom-call | tf_op jit(solution)/shard_map/pick/pallas_call | solution.py:450
  16.8 3.7 %all-to-all-start.1 = ((bf16[16,32,1024]{2,1,0:T(8,128)(2,1)}), bf16[16,32,1024]{2,1,0:T(8,128)(2,1)S(1)}, u32[]{:S(2)}, u32[]{:S(2)}) async-start(bf16[16,32,1024]{2,1,0:T(8,128)(2,1)} %pick.1), calls=%async_computation.1 | async-start | bytes 2097152 | tf_op jit(solution)/shard_map/all_to_all | solution.py:459
  21.1 1.4 %copy.13 = s32[48,2]{1,0:T(8,128)} copy(s32[48,2]{0,1:T(2,128)} %param.13) | data formatting | bytes 768 | tf_op args[3]
  22.4 1.4 %reshape.11.pairs_ref = s32[96]{0:T(128)} reshape(s32[48,2]{1,0:T(8,128)} %copy.13) | data formatting | bytes 768 | tf_op jit(solution)/shard_map/reshape | solution.py:461
  23.8 0.0 copy-done.8
  23.8 0.8 copy.12
  24.6 1.1 %reshape.10.offsets_ref = s32[768]{0:T(1024)S(1)} reshape(s32[256,3]{1,0:T(8,128)} %copy.12) | data formatting | bytes 6144 | tf_op jit(solution)/shard_map/reshape | solution.py:461
  25.7 17.6 %all-to-all-done.1.in_ref = bf16[16,32,1024]{2,1,0:T(8,128)(2,1)S(1)} async-done(((bf16[16,32,1024]{2,1,0:T(8,128)(2,1)}), bf16[16,32,1024]{2,1,0:T(8,128)(2,1)S(1)}, u32[]{:S(2)}, u32[]{:S(2)}) %all-to-all-start.1) | async-done | bytes 1048608 | tf_op jit(solution)/shard_map/all_to_all | solution.py:459
  43.3 0.0 copy-done
  43.3 0.0 copy-done.4
  43.3 0.0 copy-done.6
  43.3 0.0 copy-start.5
  43.4 0.9 copy-done.5
  44.2 0.0 copy-start.7
  44.2 0.6 copy-done.7
  44.8 13.2 %solve.1 = s16[16,272,128]{2,1,0:T(8,128)(2,1)S(1)} custom-call(s32[16]{0:T(128)S(1)} %bitcast.2, s32[768]{0:T(1024)S(1)} %reshape.10.offsets_ref, s32[96]{0:T(128)S(1)} %copy-done.7, s32[1]{0:T(128)S(6)} %copy.14.count_ref, bf16[16,32,1024]{2,1,0:T(8,128)(2,1)S(1)} %all-to-all-done.1.in_ref, bf16[256,768]{1,0:T(8,128)(2,1)S(1)} %copy-done.4, ...), custom_call_target="tpu_custom_call" | custom-call | tf_op jit(solution)/shard_map/solve/pallas_call | solution.py:398
  58.1 0.0 copy-start.2
  58.1 35.3 %all_to_all.15.in_ref.code_ref = s16[16,272,128]{2,1,0:T(8,128)(2,1)S(1)} all-to-all(s16[16,272,128]{2,1,0:T(8,128)(2,1)S(1)} %solve.1), channel_id=1, replica_groups=mesh['groups'=2,'orb'=16] {'orb'}, dimensions={0} | all-to-all | bytes 2228224 | tf_op jit(solution)/shard_map/all_to_all | solution.py:463
  93.3 0.0 copy-done.2
  93.3 4.1 %final.1 = f32[16,32768]{1,0:T(8,128)} custom-call(s32[16,1,128]{2,1,0:T(1,128)S(1)} %all-to-all-done.asked_ref, s16[16,272,128]{2,1,0:T(8,128)(2,1)S(1)} %all_to_all.15.in_ref.code_ref, s16[16,272,128]{2,1,0:T(8,128)(2,1)S(1)} %all_to_all.15.in_ref.code_ref, bf16[2,512,512]{2,1,0:T(8,128)(2,1)S(1)} %copy-done.2), custom_call_target="tpu_custom_call" | custom-call | tf_op jit(solution)/shard_map/final/pallas_call | solution.py:464
Async XLA Ops:
  1.3 13.7 %all-to-all-start = ((s32[16,1,128]{2,1,0:T(1,128)}), s32[16,1,128]{2,1,0:T(1,128)S(1)}, u32[]{:S(2)}, u32[]{:S(2)}) async-start(s32[16,1,128]{2,1,0:T(1,128)} %ask.1), calls=%async_computation | async-start | bytes 16384 | tf_op jit(solution)/shard_map/all_to_all | solution.py:449
  8.7 1.2 %copy-start.1 = (bf16[16,32768]{1,0:T(8,128)(2,1)S(1)}, bf16[16,32768]{1,0:T(8,128)(2,1)}, u32[]{:S(2)}) copy-start(bf16[16,32768]{1,0:T(8,128)(2,1)} %phi_ref.1) | copy-start | bytes 3145732
  9.9 1.0 %copy-start.3 = (bf16[512,512]{1,0:T(8,128)(2,1)S(1)}, bf16[512,512]{1,0:T(8,128)(2,1)}, u32[]{:S(2)}) copy-start(bf16[512,512]{1,0:T(8,128)(2,1)} %constant.10.clone.table_ref) | copy-start | bytes 1572868
  11.8 12.0 %copy-start.8 = (s32[256,3]{0,1:T(4,128)S(1)}, s32[256,3]{0,1:T(4,128)}, u32[]{:S(2)}) copy-start(s32[256,3]{0,1:T(4,128)} %param.11) | copy-start | bytes 9220
  11.8 31.5 %copy-start = (bf16[2,4,512,256]{3,2,1,0:T(8,128)(2,1)S(1)}, bf16[2,4,512,256]{3,2,1,0:T(8,128)(2,1)}, u32[]{:S(2)}) copy-start(bf16[2,4,512,256]{3,2,1,0:T(8,128)(2,1)} %constant.12.clone.sine_hbm) | copy-start | bytes 6291460
  11.8 31.5 %copy-start.4 = (bf16[256,768]{1,0:T(8,128)(2,1)S(1)}, bf16[256,768]{1,0:T(8,128)(2,1)}, u32[]{:S(2)}) copy-start(bf16[256,768]{1,0:T(8,128)(2,1)} %constant.11.clone.var_ref) | copy-start | bytes 1179652
  11.8 31.5 %copy-start.6 = (s32[1,16]{1,0:T(1,128)S(1)}, s32[1,16]{1,0:T(1,128)}, u32[]{:S(2)}) copy-start(s32[1,16]{1,0:T(1,128)} %param.12) | copy-start | bytes 196
  16.8 26.6 %all-to-all-start.1 = ((bf16[16,32,1024]{2,1,0:T(8,128)(2,1)}), bf16[16,32,1024]{2,1,0:T(8,128)(2,1)S(1)}, u32[]{:S(2)}, u32[]{:S(2)}) async-start(bf16[16,32,1024]{2,1,0:T(8,128)(2,1)} %pick.1), calls=%async_computation.1 | async-start | bytes 2097152 | tf_op jit(solution)/shard_map/all_to_all | solution.py:459
  43.3 0.9 copy-start.5
  44.2 0.6 copy-start.7
  58.1 35.3 %copy-start.2 = (bf16[2,512,512]{2,1,0:T(8,128)(2,1)S(1)}, bf16[2,512,512]{2,1,0:T(8,128)(2,1)}, u32[]{:S(2)}) copy-start(bf16[2,512,512]{2,1,0:T(8,128)(2,1)} %constant.14.clone.table_ref) | copy-start | bytes 3145732

commit v5 on v4

--- a/solution.py
+++ b/solution.py
@@ -33,26 +33,23 @@
     half = length // 2
     area = half * half
     count = np.arange(length) + 1.0
-    sine = np.sqrt(2.0 / (length + 1)) * np.sin(np.pi * np.outer(count, count) / (length + 1))
     eigen = 2.0 - 2.0 * np.cos(np.pi * count / (length + 1))
-    fold = [sine[parity::2, :half].T for parity in (0, 1)]
-    forward, backward, factors = [], [], []
+    modes = [eigen[0::2][::-1], eigen[1::2]]
+    near = np.arange(half) + 1.0
+    sine = np.sqrt(2.0 / (length + 1)) * np.sin(2.0 * np.pi * np.outer(near, near) / (length + 1))
+    high, low = split_bf16(np.kron(sine, sine))
+    sines = np.concatenate([high, high, low], axis=0)
+    factors = []
     for par_y in (0, 1):
         for par_z in (0, 1):
-            table = np.kron(fold[par_y], fold[par_z])
-            high, low = split_bf16(table)
-            forward.append(np.concatenate([high, low], axis=0))
-            high, low = split_bf16(table.T)
-            backward.append(np.concatenate([high, low], axis=0))
-            beta = 2.0 + (eigen[par_y::2][:, None] + eigen[par_z::2][None, :]).reshape(area)
+            beta = 2.0 + (modes[par_y][:, None] + modes[par_z][None, :]).reshape(area)
             rows = [1.0 / beta]
             for _ in range(half - 1):
                 rows.append(1.0 / (beta - rows[-1]))
             rows.append(1.0 / (1.0 - rows[-1] ** 2))
             rows.extend([rows[-1]] * 7)
             rows = np.stack(rows).astype(np.float32)
-            factors.append(rows[:, : area // 2])
-            factors.append(rows[:, area // 2 :])
+            factors.append(rows)
     place = np.arange(area)
     low_y, low_z = place // half, place % half
     variants = []
@@ -67,20 +64,24 @@
     pack = np.zeros((wide, wide), ml_dtypes.bfloat16)
     z_half, rest = spot // area, spot % area
     pack[(rest // half) * length + z_half * half + rest % half, spot] = 1
+    spot = np.arange(area)
+    z_half, rest = spot // (area // 2), spot % (area // 2)
     unpack = []
     for par_y in (0, 1):
-        y_nat = half - 1 - rest // half if par_y else rest // half
+        y_nat = half // 2 - 1 - rest // half if par_y else rest // half
         z_nat = np.where(z_half == 1, length - 1 - rest % half, rest % half)
-        one_hot = np.zeros((wide, wide), ml_dtypes.bfloat16)
+        one_hot = np.zeros((area, area), ml_dtypes.bfloat16)
         one_hot[spot, y_nat * length + z_nat] = 1
         unpack.append(one_hot)
-    return dict(
-        sines=np.stack([np.stack(forward), np.stack(backward)]),
-        factors=np.stack(factors),
-        variants=np.concatenate(variants, axis=1),
-        pack=pack,
-        unpack=np.stack(unpack),
+    left = np.concatenate(factors).astype(np.float64)
+    pieces = []
+    for _ in range(3):
+        pieces.append(left.astype(ml_dtypes.bfloat16))
+        left = left - pieces[-1].astype(np.float64)
+    variants = np.concatenate(
+        [np.concatenate(variants, axis=1), np.concatenate(pieces, axis=1)], axis=0
     )
+    return dict(sines=sines, variants=variants, pack=pack, unpack=np.stack(unpack))
 
 
 def halves(value):
@@ -128,32 +129,32 @@
 
 
 def solve_kernel(
-    orbs, fetch_ref, offsets_ref, pairs_ref, count_ref, in_ref, var_ref, sine_hbm, fac_hbm,
-    out_ref, octs, even_work, odd_work, totals, plan, used, fwd_ref, bwd_ref, fac_ref, sems,
+    orbs, slots, ints_ref, in_ref, var_ref, sine_hbm,
+    out_ref, octs, even_work, odd_work, totals, plan, used, sine_ref, fac_ref, signs, sem,
 ):
     nodes, length = in_ref.shape[0], in_ref.shape[1]
     half = length // 2
     area = half * half
     zero_at = nodes * 32
     group = 8
-    area_rows = [pl.ds(0, area), pl.ds(area, area), pl.ds(2 * area, area)]
-    moves = [(fac_hbm, fac_ref)]
-    for way, target in enumerate((fwd_ref, bwd_ref)):
-        for part in range(3):
-            source = sine_hbm.at[way, :, area_rows[part // 2], :]
-            moves.append((source, target.at[:, area_rows[part], :]))
-    tables = [pltpu.make_async_copy(*move, sems.at[k]) for k, move in enumerate(moves)]
-    for table in tables:
-        table.start()
+    table = pltpu.make_async_copy(sine_hbm, sine_ref, sem)
+    table.start()
+    row_at = lax.broadcasted_iota(jnp.int32, (half, area), 1)
+    turn_z = 1.0 - 2.0 * (row_at % 2).astype(F32)
+    turn_y = 1.0 - 2.0 * (row_at // half % 2).astype(F32)
+    signs[0] = turn_y * turn_z
+    signs[1] = turn_y
+    signs[2] = turn_z
     octs[zero_at] = jnp.zeros((half, area), BF16)
-    live_count = count_ref[0]
-    last_slot = pairs_ref.shape[0] // 2 - 1
+    fetch_at, offset_at, pair_at = 1, 1 + nodes, 1 + nodes + nodes * orbs * 3
+    live_count = ints_ref[0]
+    last_slot = slots - 1
 
     def make_variants(step, carry):
         for quad in range(4):
             block = in_ref[pl.ds(step * group, group), :, quad * area : (quad + 1) * area]
             turned = jnp.dot(
-                block.reshape(group * length, area), var_ref[...], preferred_element_type=F32
+                block.reshape(group * length, area), var_ref[:area, :], preferred_element_type=F32
             ).astype(BF16)
             for one in range(group):
                 for hx in range(2):
@@ -183,10 +184,10 @@
 
     def multiply(work, slot, t):
         at = jnp.minimum(slot, last_slot)
-        first, second = pairs_ref[2 * at], pairs_ref[2 * at + 1]
-        id_a = first * orbs + jnp.maximum(fetch_ref[first], 0)
-        id_b = second * orbs + jnp.maximum(fetch_ref[second], 0)
-        shift = [offsets_ref[id_a * 3 + k] - offsets_ref[id_b * 3 + k] for k in range(3)]
+        first, second = ints_ref[pair_at + 2 * at], ints_ref[pair_at + 2 * at + 1]
+        id_a = first * orbs + jnp.maximum(ints_ref[fetch_at + first], 0)
+        id_b = second * orbs + jnp.maximum(ints_ref[fetch_at + second], 0)
+        shift = [ints_ref[offset_at + id_a * 3 + k] - ints_ref[offset_at + id_b * 3 + k] for k in range(3)]
         fits = [[(side + shift[k] >= 0) & (side + shift[k] < 2) for side in range(2)] for k in range(3)]
         start = second * 32 + shift[0] * 16 + shift[1] * 8 + shift[2] * 4
         live = slot < live_count
@@ -204,7 +205,12 @@
                 dens.append(own * octs[spot].astype(F32))
             even0, odd0 = dens[0] + dens[1], dens[0] - dens[1]
             even1, odd1 = dens[2] + dens[3], dens[2] - dens[3]
-            folded = (even0 + even1, odd0 + odd1, even0 - even1, odd0 - odd1)
+            folded = (
+                (even0 + even1) * signs[0],
+                (odd0 + odd1) * signs[1],
+                (even0 - even1) * signs[2],
+                odd0 - odd1,
+            )
             for cls in range(4):
                 for lh in range(2):
                     work[cls * 2 + lh, pl.ds(hx * half * PITCH + t, half, stride=PITCH), :] = folded[cls][
@@ -220,7 +226,8 @@
                 pieces = [
                     work[cls * 2 + lh, pl.ds(hx * half * PITCH + t, half, stride=PITCH), :] for lh in range(2)
                 ]
-                folded.append(jnp.concatenate(pieces, axis=1))
+                piece = jnp.concatenate(pieces, axis=1)
+                folded.append(piece * signs[cls] if cls < 3 else piece)
             sum0, dif0 = folded[0] + folded[1], folded[0] - folded[1]
             sum1, dif1 = folded[2] + folded[3], folded[2] - folded[3]
             potential = (sum0 + sum1, dif0 + dif1, sum0 - sum1, dif0 - dif1)
@@ -228,7 +235,7 @@
                 moved = octs[plan[note + 1 + hx * 4 + pos]].astype(F32)
                 totals[first + (hx * 4 + pos)] += potential[pos] * moved
 
-    def begin(work, cls, table_ref):
+    def begin(work, cls):
         both = jnp.concatenate(
             [
                 jnp.concatenate(
@@ -240,7 +247,7 @@
         )
         high, low = halves(both)
         return jnp.dot(
-            jnp.concatenate([high, low, high], axis=1), table_ref[cls], preferred_element_type=F32
+            jnp.concatenate([high, low, high], axis=1), sine_ref[...], preferred_element_type=F32
         )
 
     def finish(work, cls, result):
@@ -286,14 +293,14 @@
     def half_step(work, other, before, after):
         share = BLOCK // 4
         for cls in range(4):
-            result = begin(work, cls, fwd_ref)
+            result = begin(work, cls)
             for t in range(cls * share, (cls + 1) * share):
                 gather(other, before * BLOCK + t, t)
             if cls == 2:
                 sweep(work, range(4))
             finish(work, cls, result)
         for cls in range(4):
-            result = begin(work, cls, bwd_ref)
+            result = begin(work, cls)
             if cls == 0:
                 sweep(work, range(4, 8))
             for t in range(cls * share, (cls + 1) * share):
@@ -302,8 +309,13 @@
 
     for t in range(BLOCK):
         multiply(even_work, t, t)
-    for table in tables:
-        table.wait()
+    table.wait()
+    steps = fac_ref.shape[1]
+    terms = [var_ref[area:, k * area : (k + 1) * area].astype(F32) for k in range(3)]
+    joined = (terms[2] + terms[1]) + terms[0]
+    for ch in range(8):
+        first, lanes = ch // 2 * steps, ch % 2 * 128
+        fac_ref[ch] = joined[first : first + steps, lanes : lanes + 128]
 
     def run_pair(step, carry):
         half_step(even_work, odd_work, 2 * step - 1, 2 * step + 1)
@@ -369,16 +381,18 @@
 
     lax.fori_loop(0, nodes, add_one, 0)
     for py in range(2):
-        rows = jnp.concatenate([totals[py * 4 + j] for j in range(4)], axis=1)
-        high, low = halves(rows)
-        result = jnp.dot(high, table_ref[py], preferred_element_type=F32) + jnp.dot(
-            low, table_ref[py], preferred_element_type=F32
-        )
-        for j in range(4):
-            for orb in range(orbs):
-                work[py * 4 + j, orb * pitch : orb * pitch + half, :] = result[
-                    orb * half : (orb + 1) * half, j * 128 : (j + 1) * 128
-                ]
+        for m in range(2):
+            rows = jnp.concatenate([totals[py * 4 + m], totals[py * 4 + 2 + m]], axis=1)
+            high, low = halves(rows)
+            result = jnp.dot(high, table_ref[py], preferred_element_type=F32) + jnp.dot(
+                low, table_ref[py], preferred_element_type=F32
+            )
+            first = py * 4 + 2 * (1 - m if py else m)
+            for j in range(2):
+                for orb in range(orbs):
+                    work[first + j, orb * pitch : orb * pitch + half, :] = result[
+                        orb * half : (orb + 1) * half, j * 128 : (j + 1) * 128
+                    ]
     for x in range(half):
         for j in range(plane // 128):
             out_ref[:, x * plane + j * 128 : x * plane + (j + 1) * 128] = work[
@@ -396,9 +410,9 @@
     work = pltpu.VMEM((8, length * PITCH, 128), F32)
     steps = (pairs.shape[0] // 2 + 2 * BLOCK - 1) // (2 * BLOCK)
     return pl.pallas_call(
-        functools.partial(solve_kernel, orbs),
+        functools.partial(solve_kernel, orbs, pairs.shape[0] // 2),
         out_shape=jax.ShapeDtypeStruct((nodes, 16 * half + 16, 128), jnp.int16),
-        in_specs=[smem] * 4 + [pl.BlockSpec(memory_space=pltpu.VMEM)] * 2 + [hbm] * 2,
+        in_specs=[smem] + [pl.BlockSpec(memory_space=pltpu.VMEM)] * 2 + [hbm],
         out_specs=pl.BlockSpec(memory_space=pltpu.VMEM),
         scratch_shapes=[
             pltpu.VMEM((nodes * 32 + 1, half, area), BF16),
@@ -407,16 +421,15 @@
             pltpu.VMEM((nodes * 8, half, area), F32),
             pltpu.SMEM(((2 * steps + 2) * BLOCK * 9,), jnp.int32),
             pltpu.SMEM((nodes,), jnp.int32),
-            pltpu.VMEM((4, 3 * area, area), BF16),
-            pltpu.VMEM((4, 3 * area, area), BF16),
+            pltpu.VMEM((3 * area, area), BF16),
             pltpu.VMEM((8, half + 8, 128), F32),
-            pltpu.SemaphoreType.DMA((7,)),
+            pltpu.VMEM((3, half, area), F32),
+            pltpu.SemaphoreType.DMA,
         ],
         compiler_params=pltpu.CompilerParams(vmem_limit_bytes=(10 << 20) + nodes * (704 << 10)),
         name="solve",
     )(
-        fetch, offsets, pairs, count, incoming,
-        tables["variants"], tables["sines"], tables["factors"],
+        jnp.concatenate([count, fetch, offsets, pairs]), incoming, tables["variants"], tables["sines"]
     )
 
 
@@ -469,7 +482,7 @@
             smem,
             pl.BlockSpec((nodes, 8 * half, 128), lambda hx: (0, hx, 0)),
             pl.BlockSpec((nodes, 16, 128), lambda hx: (0, half, 0)),
-            pl.BlockSpec((2, plane // 2, plane // 2), lambda hx: (0, 0, 0)),
+            pl.BlockSpec((2, plane // 4, plane // 4), lambda hx: (0, 0, 0)),
         ],
         out_specs=pl.BlockSpec((orbs, volume // 2), lambda hx: (0, hx)),
         scratch_shapes=[

time: 98 us -> 95.2 us (0.971)
  local copies, waits for them, and re-layouts: 8.41 us -> 2.85 us
  waiting for transfers between devices: 20.8 us -> 24.8 us
    all_to_all x1, waiting for transfers between devices: 17.6 us -> 21.6 us  [on_device(): lax.all_to_all(outgoing, 'orb', split_axis=0, concat_axis=0, tiled=True)]
    unnamed x20 -> x18, local copies, waits for them, and re-layouts: 5.94 us -> 2.53 us
    reshape x1, local copies, waits for them, and re-layouts: 1.37 us -> 0.12 us  [on_device(): task_pairs.reshape(-1)]
  transfers between devices with their start and end apart: 2 -> 2, of which waited for: 2 -> 2; matrix products, arithmetic and copies ran while one was open for 5% -> 1% of each run, Pallas kernels for 1% -> 1%
where the time goes in v5:
time: 95.2 us; the launch traced here: 95.5 us
  blocking collectives  35.2 us (37%)
  waiting for transfers between devices  24.8 us (26%)
  Pallas kernels  20.6 us (22%)
  starting transfers between devices  11.2 us (12%)
  local copies, waits for them, and re-layouts  2.85 us (3%)
    all_to_all x1, blocking collectives, on_device(): lax.all_to_all(partial, 'orb', split_axis=0, concat_axis=0, tiled=True)  35.2 us
    all_to_all x1, waiting for transfers between devices, on_device(): lax.all_to_all(outgoing, 'orb', split_axis=0, concat_axis=0, tiled=True)  21.6 us
    pallas_call x1, Pallas kernels, call_solve(): pl.pallas_call(functools.partial(solve_kernel, orbs, pairs.shape[0] // 2)...  13.1 us
    all_to_all x1, starting transfers between devices, on_device(): lax.all_to_all(asking, 'orb', split_axis=0, concat_axis=0, tiled=True)  7.39 us
    all_to_all x1, starting transfers between devices, on_device(): lax.all_to_all(outgoing, 'orb', split_axis=0, concat_axis=0, tiled=True)  3.8 us
    pallas_call x1, Pallas kernels, on_device(): pl.pallas_call(final_kernel, grid=(2,), out_shape=jax.ShapeDtypeStruct((o...  3.57 us
    all_to_all x1, waiting for transfers between devices, on_device(): lax.all_to_all(asking, 'orb', split_axis=0, concat_axis=0, tiled=True)  3.22 us
    unnamed x18, local copies, waits for them, and re-layouts  2.53 us
  transfers between devices with their start and end apart: 2, of which 2 were waited for; matrix products, arithmetic and copies ran while one was open for 1% of the time, Pallas kernels for 1%

profile of v5, /device:TPU:0, one launch (start us, length us, event | category | flops | bytes accessed | tf_op | source)
XLA Modules:
  0.0 95.5 jit_solution(18212082829658411847)
XLA Ops:
  0.0 1.3 %ask.1 = s32[16,1,128]{2,1,0:T(1,128)} custom-call(s32[16]{0:T(128)} %bitcast.1), custom_call_target="tpu_custom_call" | custom-call | tf_op jit(solution)/shard_map/ask/pallas_call | solution.py:446
  1.3 7.4 %all-to-all-start = ((s32[16,1,128]{2,1,0:T(1,128)}), s32[16,1,128]{2,1,0:T(1,128)S(1)}, u32[]{:S(2)}, u32[]{:S(2)}) async-start(s32[16,1,128]{2,1,0:T(1,128)} %ask.1), calls=%async_computation | async-start | bytes 16384 | tf_op jit(solution)/shard_map/all_to_all | solution.py:462
  8.7 0.0 copy-start
  8.7 1.2 %copy-done = bf16[16,32768]{1,0:T(8,128)(2,1)S(1)} copy-done((bf16[16,32768]{1,0:T(8,128)(2,1)S(1)}, bf16[16,32768]{1,0:T(8,128)(2,1)}, u32[]{:S(2)}) %copy-start) | copy-done | bytes 1048600
  9.9 0.0 copy-start.2
  9.9 1.0 %copy-done.2 = bf16[512,512]{1,0:T(8,128)(2,1)S(1)} copy-done((bf16[512,512]{1,0:T(8,128)(2,1)S(1)}, bf16[512,512]{1,0:T(8,128)(2,1)}, u32[]{:S(2)}) %copy-start.2) | copy-done | bytes 524312
  10.9 0.8 pack.1.packed_ref
  11.8 3.2 %all-to-all-done.asked_ref = s32[16,1,128]{2,1,0:T(1,128)S(1)} async-done(((s32[16,1,128]{2,1,0:T(1,128)}), s32[16,1,128]{2,1,0:T(1,128)S(1)}, u32[]{:S(2)}, u32[]{:S(2)}) %all-to-all-start) | async-done | bytes 8224 | tf_op jit(solution)/shard_map/all_to_all | solution.py:462
  15.0 1.8 %pick.1 = bf16[16,32,1024]{2,1,0:T(8,128)(2,1)} custom-call(s32[16,1,128]{2,1,0:T(1,128)S(1)} %all-to-all-done.asked_ref, bf16[16,32,1024]{2,1,0:T(8,128)(2,1)S(1)} %pack.1.packed_ref), custom_call_target="tpu_custom_call" | custom-call | tf_op jit(solution)/shard_map/pick/pallas_call | solution.py:463
  16.8 0.0 copy-start.7
  16.8 0.0 copy-start.5
  16.8 0.0 copy-start.6
  16.8 0.0 copy-start.1
  16.8 0.0 copy-start.3
  16.8 3.8 %all-to-all-start.1 = ((bf16[16,32,1024]{2,1,0:T(8,128)(2,1)}), bf16[16,32,1024]{2,1,0:T(8,128)(2,1)S(1)}, u32[]{:S(2)}, u32[]{:S(2)}) async-start(bf16[16,32,1024]{2,1,0:T(8,128)(2,1)} %pick.1), calls=%async_computation.1 | async-start | bytes 2097152 | tf_op jit(solution)/shard_map/all_to_all | solution.py:472
  21.3 0.0 copy-done.7
  21.3 0.1 copy.12
  21.4 0.1 reshape.11
  21.5 0.0 copy-done.5
  21.5 0.1 copy.11
  21.7 0.2 reshape.10
  21.9 0.0 copy-done.6
  21.9 0.1 pad_add_fusion.ints_ref
  22.0 21.6 %all-to-all-done.1.in_ref = bf16[16,32,1024]{2,1,0:T(8,128)(2,1)S(1)} async-done(((bf16[16,32,1024]{2,1,0:T(8,128)(2,1)}), bf16[16,32,1024]{2,1,0:T(8,128)(2,1)S(1)}, u32[]{:S(2)}, u32[]{:S(2)}) %all-to-all-start.1) | async-done | bytes 1048608 | tf_op jit(solution)/shard_map/all_to_all | solution.py:472
  43.5 0.0 copy-done.1
  43.5 0.0 copy-done.3
  43.5 13.1 %solve.1 = s16[16,272,128]{2,1,0:T(8,128)(2,1)S(1)} custom-call(s32[881]{0:T(1024)S(1)} %pad_add_fusion.ints_ref, bf16[16,32,1024]{2,1,0:T(8,128)(2,1)S(1)} %all-to-all-done.1.in_ref, bf16[352,768]{1,0:T(8,128)(2,1)S(1)} %copy-done.1, bf16[768,256]{1,0:T(8,128)(2,1)S(1)} %copy-done.3), custom_call_target="tpu_custom_call" | custom-call | tf_op jit(solution)/shard_map/solve/pallas_call | solution.py:412
  56.7 0.0 copy-start.4
  56.7 35.2 %all_to_all.15.in_ref.code_ref = s16[16,272,128]{2,1,0:T(8,128)(2,1)S(1)} all-to-all(s16[16,272,128]{2,1,0:T(8,128)(2,1)S(1)} %solve.1), channel_id=1, replica_groups=mesh['groups'=2,'orb'=16] {'orb'}, dimensions={0} | all-to-all | bytes 2228224 | tf_op jit(solution)/shard_map/all_to_all | solution.py:476
  91.9 0.0 copy-done.4
  91.9 3.6 %final.1 = f32[16,32768]{1,0:T(8,128)} custom-call(s32[16,1,128]{2,1,0:T(1,128)S(1)} %all-to-all-done.asked_ref, s16[16,272,128]{2,1,0:T(8,128)(2,1)S(1)} %all_to_all.15.in_ref.code_ref, s16[16,272,128]{2,1,0:T(8,128)(2,1)S(1)} %all_to_all.15.in_ref.code_ref, bf16[2,256,256]{2,1,0:T(8,128)(2,1)S(1)} %copy-done.4), custom_call_target="tpu_custom_call" | custom-call | tf_op jit(solution)/shard_map/final/pallas_call | solution.py:477
Async XLA Ops:
  1.3 13.7 %all-to-all-start = ((s32[16,1,128]{2,1,0:T(1,128)}), s32[16,1,128]{2,1,0:T(1,128)S(1)}, u32[]{:S(2)}, u32[]{:S(2)}) async-start(s32[16,1,128]{2,1,0:T(1,128)} %ask.1), calls=%async_computation | async-start | bytes 16384 | tf_op jit(solution)/shard_map/all_to_all | solution.py:462
  8.7 1.2 %copy-start = (bf16[16,32768]{1,0:T(8,128)(2,1)S(1)}, bf16[16,32768]{1,0:T(8,128)(2,1)}, u32[]{:S(2)}) copy-start(bf16[16,32768]{1,0:T(8,128)(2,1)} %phi_ref.1) | copy-start | bytes 3145732
  9.9 1.0 %copy-start.2 = (bf16[512,512]{1,0:T(8,128)(2,1)S(1)}, bf16[512,512]{1,0:T(8,128)(2,1)}, u32[]{:S(2)}) copy-start(bf16[512,512]{1,0:T(8,128)(2,1)} %constant.8.clone.table_ref) | copy-start | bytes 1572868
  16.8 4.5 %copy-start.7 = (s32[48,2]{0,1:T(2,128)S(1)}, s32[48,2]{0,1:T(2,128)}, u32[]{:S(2)}) copy-start(s32[48,2]{0,1:T(2,128)} %param.12) | copy-start | bytes 1156
  16.8 4.7 %copy-start.5 = (s32[256,3]{0,1:T(4,128)S(1)}, s32[256,3]{0,1:T(4,128)}, u32[]{:S(2)}) copy-start(s32[256,3]{0,1:T(4,128)} %param.10) | copy-start | bytes 9220
  16.8 5.1 %copy-start.6 = (s32[1,16]{1,0:T(1,128)S(1)}, s32[1,16]{1,0:T(1,128)}, u32[]{:S(2)}) copy-start(s32[1,16]{1,0:T(1,128)} %param.11) | copy-start | bytes 196
  16.8 26.7 %copy-start.1 = (bf16[352,768]{1,0:T(8,128)(2,1)S(1)}, bf16[352,768]{1,0:T(8,128)(2,1)}, u32[]{:S(2)}) copy-start(bf16[352,768]{1,0:T(8,128)(2,1)} %constant.9.clone.var_ref) | copy-start | bytes 1622020
  16.8 26.7 %copy-start.3 = (bf16[768,256]{1,0:T(8,128)(2,1)S(1)}, bf16[768,256]{1,0:T(8,128)(2,1)}, u32[]{:S(2)}) copy-start(bf16[768,256]{1,0:T(8,128)(2,1)} %constant.10.clone.sine_hbm) | copy-start | bytes 1179652
  16.8 26.7 %all-to-all-start.1 = ((bf16[16,32,1024]{2,1,0:T(8,128)(2,1)}), bf16[16,32,1024]{2,1,0:T(8,128)(2,1)S(1)}, u32[]{:S(2)}, u32[]{:S(2)}) async-start(bf16[16,32,1024]{2,1,0:T(8,128)(2,1)} %pick.1), calls=%async_computation.1 | async-start | bytes 2097152 | tf_op jit(solution)/shard_map/all_to_all | solution.py:472
  56.7 35.3 %copy-start.4 = (bf16[2,256,256]{2,1,0:T(8,128)(2,1)S(1)}, bf16[2,256,256]{2,1,0:T(8,128)(2,1)}, u32[]{:S(2)}) copy-start(bf16[2,256,256]{2,1,0:T(8,128)(2,1)} %constant.11.clone.table_ref) | copy-start | bytes 786436

commit v6 on v5

--- a/solution.py
+++ b/solution.py
@@ -130,7 +130,7 @@
 
 def solve_kernel(
     orbs, slots, ints_ref, in_ref, var_ref, sine_hbm,
-    out_ref, octs, even_work, odd_work, totals, plan, used, sine_ref, fac_ref, signs, sem,
+    out_ref, octs, work, totals, plan, used, sine_ref, fac_ref, signs, sem,
 ):
     nodes, length = in_ref.shape[0], in_ref.shape[1]
     half = length // 2
@@ -174,13 +174,6 @@
         return carry
 
     lax.fori_loop(0, nodes, clear, 0)
-    for ch in range(8):
-        even_work[ch] = jnp.zeros(even_work.shape[1:], F32)
-        odd_work[ch] = jnp.zeros(odd_work.shape[1:], F32)
-    for t in range(BLOCK):
-        plan[t * 9] = 0
-        for k in range(8):
-            plan[t * 9 + 1 + k] = zero_at
 
     def multiply(work, slot, t):
         at = jnp.minimum(slot, last_slot)
@@ -191,7 +184,7 @@
         fits = [[(side + shift[k] >= 0) & (side + shift[k] < 2) for side in range(2)] for k in range(3)]
         start = second * 32 + shift[0] * 16 + shift[1] * 8 + shift[2] * 4
         live = slot < live_count
-        note = (slot + BLOCK) * 9
+        note = t * 9
         plan[note] = first
         used[first] = jnp.where(live, 1, used[first])
         for hx in range(2):
@@ -218,7 +211,7 @@
                     ]
 
     def gather(work, slot, t):
-        note = (slot + BLOCK) * 9
+        note = t * 9
         first = plan[note] * 8
         for hx in range(2):
             folded = []
@@ -290,25 +283,6 @@
                 work[ch, rows(x), :] = low[ch]
                 work[ch, rows(far), :] = high[ch]
 
-    def half_step(work, other, before, after):
-        share = BLOCK // 4
-        for cls in range(4):
-            result = begin(work, cls)
-            for t in range(cls * share, (cls + 1) * share):
-                gather(other, before * BLOCK + t, t)
-            if cls == 2:
-                sweep(work, range(4))
-            finish(work, cls, result)
-        for cls in range(4):
-            result = begin(work, cls)
-            if cls == 0:
-                sweep(work, range(4, 8))
-            for t in range(cls * share, (cls + 1) * share):
-                multiply(other, after * BLOCK + t, t)
-            finish(work, cls, result)
-
-    for t in range(BLOCK):
-        multiply(even_work, t, t)
     table.wait()
     steps = fac_ref.shape[1]
     terms = [var_ref[area:, k * area : (k + 1) * area].astype(F32) for k in range(3)]
@@ -317,15 +291,21 @@
         first, lanes = ch // 2 * steps, ch % 2 * 128
         fac_ref[ch] = joined[first : first + steps, lanes : lanes + 128]
 
-    def run_pair(step, carry):
-        half_step(even_work, odd_work, 2 * step - 1, 2 * step + 1)
-        half_step(odd_work, even_work, 2 * step, 2 * step + 2)
+    def run_block(step, carry):
+        for t in range(BLOCK):
+            multiply(work, step * BLOCK + t, t)
+        for cls in range(4):
+            result = begin(work, cls)
+            finish(work, cls, result)
+        sweep(work, range(8))
+        for cls in range(4):
+            result = begin(work, cls)
+            finish(work, cls, result)
+        for t in range(BLOCK):
+            gather(work, step * BLOCK + t, t)
         return carry
 
-    pairs = (live_count + 2 * BLOCK - 1) // (2 * BLOCK)
-    lax.fori_loop(0, pairs, run_pair, 0)
-    for t in range(BLOCK):
-        gather(odd_work, (2 * pairs - 1) * BLOCK + t, t)
+    lax.fori_loop(0, (live_count + BLOCK - 1) // BLOCK, run_block, 0)
 
     def send_out(owner, carry):
         @pl.when(used[owner] == 0)
@@ -408,7 +388,6 @@
     smem = pl.BlockSpec(memory_space=pltpu.SMEM)
     hbm = pl.BlockSpec(memory_space=pl.ANY)
     work = pltpu.VMEM((8, length * PITCH, 128), F32)
-    steps = (pairs.shape[0] // 2 + 2 * BLOCK - 1) // (2 * BLOCK)
     return pl.pallas_call(
         functools.partial(solve_kernel, orbs, pairs.shape[0] // 2),
         out_shape=jax.ShapeDtypeStruct((nodes, 16 * half + 16, 128), jnp.int16),
@@ -417,9 +396,8 @@
         scratch_shapes=[
             pltpu.VMEM((nodes * 32 + 1, half, area), BF16),
             work,
-            work,
             pltpu.VMEM((nodes * 8, half, area), F32),
-            pltpu.SMEM(((2 * steps + 2) * BLOCK * 9,), jnp.int32),
+            pltpu.SMEM((BLOCK * 9,), jnp.int32),
             pltpu.SMEM((nodes,), jnp.int32),
             pltpu.VMEM((3 * area, area), BF16),
             pltpu.VMEM((8, half + 8, 128), F32),

time: 95.2 us -> 95.3 us (level)
  the two profiles are of different devices: /device:TPU:0 before, /device:TPU:3 now
where the time goes in v6:
time: 95.3 us; the launch traced here: 94.2 us
  blocking collectives  43.1 us (45%)
  waiting for transfers between devices  24.5 us (26%)
  Pallas kernels  12.1 us (13%)
  starting transfers between devices  10.8 us (11%)
  local copies, waits for them, and re-layouts  2.85 us (3%)
    all_to_all x1, blocking collectives, on_device(): lax.all_to_all(partial, 'orb', split_axis=0, concat_axis=0, tiled=True)  43.1 us
    all_to_all x1, waiting for transfers between devices, on_device(): lax.all_to_all(outgoing, 'orb', split_axis=0, concat_axis=0, tiled=True)  21.9 us
    all_to_all x1, starting transfers between devices, on_device(): lax.all_to_all(asking, 'orb', split_axis=0, concat_axis=0, tiled=True)  6.52 us
    pallas_call x1, Pallas kernels, call_solve(): pl.pallas_call(functools.partial(solve_kernel, orbs, pairs.shape[0] // 2)...  4.49 us
    all_to_all x1, starting transfers between devices, on_device(): lax.all_to_all(outgoing, 'orb', split_axis=0, concat_axis=0, tiled=True)  4.31 us
    pallas_call x1, Pallas kernels, on_device(): pl.pallas_call(final_kernel, grid=(2,), out_shape=jax.ShapeDtypeStruct((o...  3.73 us
    all_to_all x1, waiting for transfers between devices, on_device(): lax.all_to_all(asking, 'orb', split_axis=0, concat_axis=0, tiled=True)  2.6 us
    unnamed x18, local copies, waits for them, and re-layouts  2.52 us
  transfers between devices with their start and end apart: 2, of which 2 were waited for; matrix products, arithmetic and copies ran while one was open for 1% of the time, Pallas kernels for 1%

profile of v6, /device:TPU:3, one launch (start us, length us, event | category | flops | bytes accessed | tf_op | source)
XLA Modules:
  0.0 94.2 jit_solution(2154465044571709281)
XLA Ops:
  0.0 1.3 %ask.1 = s32[16,1,128]{2,1,0:T(1,128)} custom-call(s32[16]{0:T(128)} %bitcast.1), custom_call_target="tpu_custom_call" | custom-call | tf_op jit(solution)/shard_map/ask/pallas_call | solution.py:424
  1.3 6.5 %all-to-all-start = ((s32[16,1,128]{2,1,0:T(1,128)}), s32[16,1,128]{2,1,0:T(1,128)S(1)}, u32[]{:S(2)}, u32[]{:S(2)}) async-start(s32[16,1,128]{2,1,0:T(1,128)} %ask.1), calls=%async_computation | async-start | bytes 16384 | tf_op jit(solution)/shard_map/all_to_all | solution.py:440
  7.8 0.0 copy-start
  7.8 1.2 %copy-done = bf16[16,32768]{1,0:T(8,128)(2,1)S(1)} copy-done((bf16[16,32768]{1,0:T(8,128)(2,1)S(1)}, bf16[16,32768]{1,0:T(8,128)(2,1)}, u32[]{:S(2)}) %copy-start) | copy-done | bytes 1048600
  9.0 0.0 copy-start.2
  9.0 1.0 %copy-done.2 = bf16[512,512]{1,0:T(8,128)(2,1)S(1)} copy-done((bf16[512,512]{1,0:T(8,128)(2,1)S(1)}, bf16[512,512]{1,0:T(8,128)(2,1)}, u32[]{:S(2)}) %copy-start.2) | copy-done | bytes 524312
  10.1 0.8 pack.1.packed_ref
  10.9 2.6 %all-to-all-done.asked_ref = s32[16,1,128]{2,1,0:T(1,128)S(1)} async-done(((s32[16,1,128]{2,1,0:T(1,128)}), s32[16,1,128]{2,1,0:T(1,128)S(1)}, u32[]{:S(2)}, u32[]{:S(2)}) %all-to-all-start) | async-done | bytes 8224 | tf_op jit(solution)/shard_map/all_to_all | solution.py:440
  13.5 1.8 %pick.1 = bf16[16,32,1024]{2,1,0:T(8,128)(2,1)} custom-call(s32[16,1,128]{2,1,0:T(1,128)S(1)} %all-to-all-done.asked_ref, bf16[16,32,1024]{2,1,0:T(8,128)(2,1)S(1)} %pack.1.packed_ref), custom_call_target="tpu_custom_call" | custom-call | tf_op jit(solution)/shard_map/pick/pallas_call | solution.py:441
  15.3 0.0 copy-start.7
  15.3 0.0 copy-start.5
  15.3 0.0 copy-start.6
  15.3 0.0 copy-start.1
  15.3 0.0 copy-start.3
  15.3 4.3 %all-to-all-start.1 = ((bf16[16,32,1024]{2,1,0:T(8,128)(2,1)}), bf16[16,32,1024]{2,1,0:T(8,128)(2,1)S(1)}, u32[]{:S(2)}, u32[]{:S(2)}) async-start(bf16[16,32,1024]{2,1,0:T(8,128)(2,1)} %pick.1), calls=%async_computation.1 | async-start | bytes 2097152 | tf_op jit(solution)/shard_map/all_to_all | solution.py:450
  20.3 0.0 copy-done.7
  20.3 0.1 copy.12
  20.4 0.1 reshape.11
  20.5 0.0 copy-done.5
  20.5 0.1 copy.11
  20.7 0.2 reshape.10
  20.9 0.0 copy-done.6
  20.9 0.1 pad_add_fusion.ints_ref
  21.0 21.9 %all-to-all-done.1.in_ref = bf16[16,32,1024]{2,1,0:T(8,128)(2,1)S(1)} async-done(((bf16[16,32,1024]{2,1,0:T(8,128)(2,1)}), bf16[16,32,1024]{2,1,0:T(8,128)(2,1)S(1)}, u32[]{:S(2)}, u32[]{:S(2)}) %all-to-all-start.1) | async-done | bytes 1048608 | tf_op jit(solution)/shard_map/all_to_all | solution.py:450
  42.8 0.0 copy-done.1
  42.8 0.0 copy-done.3
  42.8 4.5 %solve.1 = s16[16,272,128]{2,1,0:T(8,128)(2,1)S(1)} custom-call(s32[881]{0:T(1024)S(1)} %pad_add_fusion.ints_ref, bf16[16,32,1024]{2,1,0:T(8,128)(2,1)S(1)} %all-to-all-done.1.in_ref, bf16[352,768]{1,0:T(8,128)(2,1)S(1)} %copy-done.1, bf16[768,256]{1,0:T(8,128)(2,1)S(1)} %copy-done.3), custom_call_target="tpu_custom_call" | custom-call | tf_op jit(solution)/shard_map/solve/pallas_call | solution.py:391
  47.3 0.0 copy-start.4
  47.3 43.1 %all_to_all.15.in_ref.code_ref = s16[16,272,128]{2,1,0:T(8,128)(2,1)S(1)} all-to-all(s16[16,272,128]{2,1,0:T(8,128)(2,1)S(1)} %solve.1), channel_id=1, replica_groups=mesh['groups'=2,'orb'=16] {'orb'}, dimensions={0} | all-to-all | bytes 2228224 | tf_op jit(solution)/shard_map/all_to_all | solution.py:454
  90.5 0.0 copy-done.4
  90.5 3.7 %final.1 = f32[16,32768]{1,0:T(8,128)} custom-call(s32[16,1,128]{2,1,0:T(1,128)S(1)} %all-to-all-done.asked_ref, s16[16,272,128]{2,1,0:T(8,128)(2,1)S(1)} %all_to_all.15.in_ref.code_ref, s16[16,272,128]{2,1,0:T(8,128)(2,1)S(1)} %all_to_all.15.in_ref.code_ref, bf16[2,256,256]{2,1,0:T(8,128)(2,1)S(1)} %copy-done.4), custom_call_target="tpu_custom_call" | custom-call | tf_op jit(solution)/shard_map/final/pallas_call | solution.py:455
Async XLA Ops:
  1.3 12.2 %all-to-all-start = ((s32[16,1,128]{2,1,0:T(1,128)}), s32[16,1,128]{2,1,0:T(1,128)S(1)}, u32[]{:S(2)}, u32[]{:S(2)}) async-start(s32[16,1,128]{2,1,0:T(1,128)} %ask.1), calls=%async_computation | async-start | bytes 16384 | tf_op jit(solution)/shard_map/all_to_all | solution.py:440
  7.8 1.2 %copy-start = (bf16[16,32768]{1,0:T(8,128)(2,1)S(1)}, bf16[16,32768]{1,0:T(8,128)(2,1)}, u32[]{:S(2)}) copy-start(bf16[16,32768]{1,0:T(8,128)(2,1)} %phi_ref.1) | copy-start | bytes 3145732
  9.0 1.0 %copy-start.2 = (bf16[512,512]{1,0:T(8,128)(2,1)S(1)}, bf16[512,512]{1,0:T(8,128)(2,1)}, u32[]{:S(2)}) copy-start(bf16[512,512]{1,0:T(8,128)(2,1)} %constant.8.clone.table_ref) | copy-start | bytes 1572868
  15.3 5.0 %copy-start.7 = (s32[48,2]{0,1:T(2,128)S(1)}, s32[48,2]{0,1:T(2,128)}, u32[]{:S(2)}) copy-start(s32[48,2]{0,1:T(2,128)} %param.12) | copy-start | bytes 1156
  15.3 5.2 %copy-start.5 = (s32[256,3]{0,1:T(4,128)S(1)}, s32[256,3]{0,1:T(4,128)}, u32[]{:S(2)}) copy-start(s32[256,3]{0,1:T(4,128)} %param.10) | copy-start | bytes 9220
  15.3 5.6 %copy-start.6 = (s32[1,16]{1,0:T(1,128)S(1)}, s32[1,16]{1,0:T(1,128)}, u32[]{:S(2)}) copy-start(s32[1,16]{1,0:T(1,128)} %param.11) | copy-start | bytes 196
  15.3 27.5 %copy-start.1 = (bf16[352,768]{1,0:T(8,128)(2,1)S(1)}, bf16[352,768]{1,0:T(8,128)(2,1)}, u32[]{:S(2)}) copy-start(bf16[352,768]{1,0:T(8,128)(2,1)} %constant.9.clone.var_ref) | copy-start | bytes 1622020
  15.3 27.5 %copy-start.3 = (bf16[768,256]{1,0:T(8,128)(2,1)S(1)}, bf16[768,256]{1,0:T(8,128)(2,1)}, u32[]{:S(2)}) copy-start(bf16[768,256]{1,0:T(8,128)(2,1)} %constant.10.clone.sine_hbm) | copy-start | bytes 1179652
  15.3 27.5 %all-to-all-start.1 = ((bf16[16,32,1024]{2,1,0:T(8,128)(2,1)}), bf16[16,32,1024]{2,1,0:T(8,128)(2,1)S(1)}, u32[]{:S(2)}, u32[]{:S(2)}) async-start(bf16[16,32,1024]{2,1,0:T(8,128)(2,1)} %pick.1), calls=%async_computation.1 | async-start | bytes 2097152 | tf_op jit(solution)/shard_map/all_to_all | solution.py:450
  47.3 43.2 %copy-start.4 = (bf16[2,256,256]{2,1,0:T(8,128)(2,1)S(1)}, bf16[2,256,256]{2,1,0:T(8,128)(2,1)}, u32[]{:S(2)}) copy-start(bf16[2,256,256]{2,1,0:T(8,128)(2,1)} %constant.11.clone.table_ref) | copy-start | bytes 786436

commit v7 on v5

--- a/solution.py
+++ b/solution.py
@@ -174,13 +174,6 @@
         return carry
 
     lax.fori_loop(0, nodes, clear, 0)
-    for ch in range(8):
-        even_work[ch] = jnp.zeros(even_work.shape[1:], F32)
-        odd_work[ch] = jnp.zeros(odd_work.shape[1:], F32)
-    for t in range(BLOCK):
-        plan[t * 9] = 0
-        for k in range(8):
-            plan[t * 9 + 1 + k] = zero_at
 
     def multiply(work, slot, t):
         at = jnp.minimum(slot, last_slot)
@@ -294,8 +287,9 @@
         share = BLOCK // 4
         for cls in range(4):
             result = begin(work, cls)
-            for t in range(cls * share, (cls + 1) * share):
-                gather(other, before * BLOCK + t, t)
+            if before is not None:
+                for t in range(cls * share, (cls + 1) * share):
+                    gather(other, before * BLOCK + t, t)
             if cls == 2:
                 sweep(work, range(4))
             finish(work, cls, result)
@@ -303,8 +297,9 @@
             result = begin(work, cls)
             if cls == 0:
                 sweep(work, range(4, 8))
-            for t in range(cls * share, (cls + 1) * share):
-                multiply(other, after * BLOCK + t, t)
+            if after is not None:
+                for t in range(cls * share, (cls + 1) * share):
+                    multiply(other, after * BLOCK + t, t)
             finish(work, cls, result)
 
     for t in range(BLOCK):
@@ -318,12 +313,14 @@
         fac_ref[ch] = joined[first : first + steps, lanes : lanes + 128]
 
     def run_pair(step, carry):
-        half_step(even_work, odd_work, 2 * step - 1, 2 * step + 1)
         half_step(odd_work, even_work, 2 * step, 2 * step + 2)
+        half_step(even_work, odd_work, 2 * step + 1, 2 * step + 3)
         return carry
 
     pairs = (live_count + 2 * BLOCK - 1) // (2 * BLOCK)
-    lax.fori_loop(0, pairs, run_pair, 0)
+    half_step(even_work, odd_work, None, 1)
+    lax.fori_loop(0, pairs - 1, run_pair, 0)
+    half_step(odd_work, even_work, 2 * pairs - 2, None)
     for t in range(BLOCK):
         gather(odd_work, (2 * pairs - 1) * BLOCK + t, t)
 

time: 95.2 us -> 94 us (0.987)
  blocking collectives: 35.2 us -> 34.1 us
  Pallas kernels: 20.6 us -> 19.6 us
    all_to_all x1, blocking collectives: 35.2 us -> 34.1 us  [on_device(): lax.all_to_all(partial, 'orb', split_axis=0, concat_axis=0, tiled=True)]
    pallas_call x1, Pallas kernels: 13.1 us -> 12.1 us  [call_solve(): pl.pallas_call(functools.partial(solve_kernel, orbs, pairs.shape[0] // 2)...]
where the time goes in v7:
time: 94 us; the launch traced here: 93.4 us
  blocking collectives  34.1 us (36%)
  waiting for transfers between devices  24.8 us (26%)
  Pallas kernels  19.6 us (21%)
  starting transfers between devices  11.2 us (12%)
  local copies, waits for them, and re-layouts  2.85 us (3%)
    all_to_all x1, blocking collectives, on_device(): lax.all_to_all(partial, 'orb', split_axis=0, concat_axis=0, tiled=True)  34.1 us
    all_to_all x1, waiting for transfers between devices, on_device(): lax.all_to_all(outgoing, 'orb', split_axis=0, concat_axis=0, tiled=True)  21.6 us
    pallas_call x1, Pallas kernels, call_solve(): pl.pallas_call(functools.partial(solve_kernel, orbs, pairs.shape[0] // 2)...  12.1 us
    all_to_all x1, starting transfers between devices, on_device(): lax.all_to_all(asking, 'orb', split_axis=0, concat_axis=0, tiled=True)  7.39 us
    all_to_all x1, starting transfers between devices, on_device(): lax.all_to_all(outgoing, 'orb', split_axis=0, concat_axis=0, tiled=True)  3.8 us
    pallas_call x1, Pallas kernels, on_device(): pl.pallas_call(final_kernel, grid=(2,), out_shape=jax.ShapeDtypeStruct((o...  3.64 us
    all_to_all x1, waiting for transfers between devices, on_device(): lax.all_to_all(asking, 'orb', split_axis=0, concat_axis=0, tiled=True)  3.22 us
    unnamed x18, local copies, waits for them, and re-layouts  2.53 us
  transfers between devices with their start and end apart: 2, of which 2 were waited for; matrix products, arithmetic and copies ran while one was open for 1% of the time, Pallas kernels for 1%

profile of v7, /device:TPU:0, one launch (start us, length us, event | category | flops | bytes accessed | tf_op | source)
XLA Modules:
  0.0 93.4 jit_solution(618480669515709397)
XLA Ops:
  0.0 1.3 %ask.1 = s32[16,1,128]{2,1,0:T(1,128)} custom-call(s32[16]{0:T(128)} %bitcast.1), custom_call_target="tpu_custom_call" | custom-call | tf_op jit(solution)/shard_map/ask/pallas_call | solution.py:443
  1.3 7.4 %all-to-all-start = ((s32[16,1,128]{2,1,0:T(1,128)}), s32[16,1,128]{2,1,0:T(1,128)S(1)}, u32[]{:S(2)}, u32[]{:S(2)}) async-start(s32[16,1,128]{2,1,0:T(1,128)} %ask.1), calls=%async_computation | async-start | bytes 16384 | tf_op jit(solution)/shard_map/all_to_all | solution.py:459
  8.7 0.0 copy-start
  8.7 1.2 %copy-done = bf16[16,32768]{1,0:T(8,128)(2,1)S(1)} copy-done((bf16[16,32768]{1,0:T(8,128)(2,1)S(1)}, bf16[16,32768]{1,0:T(8,128)(2,1)}, u32[]{:S(2)}) %copy-start) | copy-done | bytes 1048600
  9.9 0.0 copy-start.2
  9.9 1.0 %copy-done.2 = bf16[512,512]{1,0:T(8,128)(2,1)S(1)} copy-done((bf16[512,512]{1,0:T(8,128)(2,1)S(1)}, bf16[512,512]{1,0:T(8,128)(2,1)}, u32[]{:S(2)}) %copy-start.2) | copy-done | bytes 524312
  10.9 0.8 pack.1.packed_ref
  11.8 3.2 %all-to-all-done.asked_ref = s32[16,1,128]{2,1,0:T(1,128)S(1)} async-done(((s32[16,1,128]{2,1,0:T(1,128)}), s32[16,1,128]{2,1,0:T(1,128)S(1)}, u32[]{:S(2)}, u32[]{:S(2)}) %all-to-all-start) | async-done | bytes 8224 | tf_op jit(solution)/shard_map/all_to_all | solution.py:459
  15.0 1.8 %pick.1 = bf16[16,32,1024]{2,1,0:T(8,128)(2,1)} custom-call(s32[16,1,128]{2,1,0:T(1,128)S(1)} %all-to-all-done.asked_ref, bf16[16,32,1024]{2,1,0:T(8,128)(2,1)S(1)} %pack.1.packed_ref), custom_call_target="tpu_custom_call" | custom-call | tf_op jit(solution)/shard_map/pick/pallas_call | solution.py:460
  16.8 0.0 copy-start.7
  16.8 0.0 copy-start.5
  16.8 0.0 copy-start.6
  16.8 0.0 copy-start.1
  16.8 0.0 copy-start.3
  16.8 3.8 %all-to-all-start.1 = ((bf16[16,32,1024]{2,1,0:T(8,128)(2,1)}), bf16[16,32,1024]{2,1,0:T(8,128)(2,1)S(1)}, u32[]{:S(2)}, u32[]{:S(2)}) async-start(bf16[16,32,1024]{2,1,0:T(8,128)(2,1)} %pick.1), calls=%async_computation.1 | async-start | bytes 2097152 | tf_op jit(solution)/shard_map/all_to_all | solution.py:469
  21.3 0.0 copy-done.7
  21.3 0.1 copy.12
  21.4 0.1 reshape.11
  21.5 0.0 copy-done.5
  21.5 0.1 copy.11
  21.7 0.2 reshape.10
  21.9 0.0 copy-done.6
  21.9 0.1 pad_add_fusion.ints_ref
  22.0 21.6 %all-to-all-done.1.in_ref = bf16[16,32,1024]{2,1,0:T(8,128)(2,1)S(1)} async-done(((bf16[16,32,1024]{2,1,0:T(8,128)(2,1)}), bf16[16,32,1024]{2,1,0:T(8,128)(2,1)S(1)}, u32[]{:S(2)}, u32[]{:S(2)}) %all-to-all-start.1) | async-done | bytes 1048608 | tf_op jit(solution)/shard_map/all_to_all | solution.py:469
  43.5 0.0 copy-done.1
  43.5 0.0 copy-done.3
  43.5 12.1 %solve.1 = s16[16,272,128]{2,1,0:T(8,128)(2,1)S(1)} custom-call(s32[881]{0:T(1024)S(1)} %pad_add_fusion.ints_ref, bf16[16,32,1024]{2,1,0:T(8,128)(2,1)S(1)} %all-to-all-done.1.in_ref, bf16[352,768]{1,0:T(8,128)(2,1)S(1)} %copy-done.1, bf16[768,256]{1,0:T(8,128)(2,1)S(1)} %copy-done.3), custom_call_target="tpu_custom_call" | custom-call | tf_op jit(solution)/shard_map/solve/pallas_call | solution.py:409
  55.6 0.0 copy-start.4
  55.6 34.1 %all_to_all.15.in_ref.code_ref = s16[16,272,128]{2,1,0:T(8,128)(2,1)S(1)} all-to-all(s16[16,272,128]{2,1,0:T(8,128)(2,1)S(1)} %solve.1), channel_id=1, replica_groups=mesh['groups'=2,'orb'=16] {'orb'}, dimensions={0} | all-to-all | bytes 2228224 | tf_op jit(solution)/shard_map/all_to_all | solution.py:473
  89.7 0.0 copy-done.4
  89.7 3.6 %final.1 = f32[16,32768]{1,0:T(8,128)} custom-call(s32[16,1,128]{2,1,0:T(1,128)S(1)} %all-to-all-done.asked_ref, s16[16,272,128]{2,1,0:T(8,128)(2,1)S(1)} %all_to_all.15.in_ref.code_ref, s16[16,272,128]{2,1,0:T(8,128)(2,1)S(1)} %all_to_all.15.in_ref.code_ref, bf16[2,256,256]{2,1,0:T(8,128)(2,1)S(1)} %copy-done.4), custom_call_target="tpu_custom_call" | custom-call | tf_op jit(solution)/shard_map/final/pallas_call | solution.py:474
Async XLA Ops:
  1.3 13.7 %all-to-all-start = ((s32[16,1,128]{2,1,0:T(1,128)}), s32[16,1,128]{2,1,0:T(1,128)S(1)}, u32[]{:S(2)}, u32[]{:S(2)}) async-start(s32[16,1,128]{2,1,0:T(1,128)} %ask.1), calls=%async_computation | async-start | bytes 16384 | tf_op jit(solution)/shard_map/all_to_all | solution.py:459
  8.7 1.2 %copy-start = (bf16[16,32768]{1,0:T(8,128)(2,1)S(1)}, bf16[16,32768]{1,0:T(8,128)(2,1)}, u32[]{:S(2)}) copy-start(bf16[16,32768]{1,0:T(8,128)(2,1)} %phi_ref.1) | copy-start | bytes 3145732
  9.9 1.0 %copy-start.2 = (bf16[512,512]{1,0:T(8,128)(2,1)S(1)}, bf16[512,512]{1,0:T(8,128)(2,1)}, u32[]{:S(2)}) copy-start(bf16[512,512]{1,0:T(8,128)(2,1)} %constant.8.clone.table_ref) | copy-start | bytes 1572868
  16.8 4.5 %copy-start.7 = (s32[48,2]{0,1:T(2,128)S(1)}, s32[48,2]{0,1:T(2,128)}, u32[]{:S(2)}) copy-start(s32[48,2]{0,1:T(2,128)} %param.12) | copy-start | bytes 1156
  16.8 4.7 %copy-start.5 = (s32[256,3]{0,1:T(4,128)S(1)}, s32[256,3]{0,1:T(4,128)}, u32[]{:S(2)}) copy-start(s32[256,3]{0,1:T(4,128)} %param.10) | copy-start | bytes 9220
  16.8 5.1 %copy-start.6 = (s32[1,16]{1,0:T(1,128)S(1)}, s32[1,16]{1,0:T(1,128)}, u32[]{:S(2)}) copy-start(s32[1,16]{1,0:T(1,128)} %param.11) | copy-start | bytes 196
  16.8 26.7 %copy-start.1 = (bf16[352,768]{1,0:T(8,128)(2,1)S(1)}, bf16[352,768]{1,0:T(8,128)(2,1)}, u32[]{:S(2)}) copy-start(bf16[352,768]{1,0:T(8,128)(2,1)} %constant.9.clone.var_ref) | copy-start | bytes 1622020
  16.8 26.7 %copy-start.3 = (bf16[768,256]{1,0:T(8,128)(2,1)S(1)}, bf16[768,256]{1,0:T(8,128)(2,1)}, u32[]{:S(2)}) copy-start(bf16[768,256]{1,0:T(8,128)(2,1)} %constant.10.clone.sine_hbm) | copy-start | bytes 1179652
  16.8 26.7 %all-to-all-start.1 = ((bf16[16,32,1024]{2,1,0:T(8,128)(2,1)}), bf16[16,32,1024]{2,1,0:T(8,128)(2,1)S(1)}, u32[]{:S(2)}, u32[]{:S(2)}) async-start(bf16[16,32,1024]{2,1,0:T(8,128)(2,1)} %pick.1), calls=%async_computation.1 | async-start | bytes 2097152 | tf_op jit(solution)/shard_map/all_to_all | solution.py:469
  55.6 34.1 %copy-start.4 = (bf16[2,256,256]{2,1,0:T(8,128)(2,1)S(1)}, bf16[2,256,256]{2,1,0:T(8,128)(2,1)}, u32[]{:S(2)}) copy-start(bf16[2,256,256]{2,1,0:T(8,128)(2,1)} %constant.11.clone.table_ref) | copy-start | bytes 786436

commit v8 on v7

--- a/solution.py
+++ b/solution.py
@@ -59,10 +59,9 @@
         one_hot = np.zeros((area, area), ml_dtypes.bfloat16)
         one_hot[src_y * half + src_z, place] = 1
         variants.append(one_hot)
-    wide = 2 * area
-    spot = np.arange(wide)
-    pack = np.zeros((wide, wide), ml_dtypes.bfloat16)
-    z_half, rest = spot // area, spot % area
+    spot = np.arange(area)
+    z_half, rest = spot // (area // 2), spot % (area // 2)
+    pack = np.zeros((area, area), ml_dtypes.bfloat16)
     pack[(rest // half) * length + z_half * half + rest % half, spot] = 1
     spot = np.arange(area)
     z_half, rest = spot // (area // 2), spot % (area // 2)
@@ -99,18 +98,19 @@
     orbs = phi_ref.shape[0]
     length = out_ref.shape[1]
     plane = length * length
-    wide = plane // 2
     pitch = orbs + 1
-    for y_half in range(2):
+    area = plane // 4
+    for quarter in range(4):
         rows = jnp.concatenate(
-            [phi_ref[:, x * plane + y_half * wide : x * plane + (y_half + 1) * wide] for x in range(length)],
+            [phi_ref[:, x * plane + quarter * area : x * plane + (quarter + 1) * area] for x in range(length)],
             axis=0,
         )
         moved = jnp.dot(rows, table_ref[...], preferred_element_type=F32)
-        for j in range(wide // 128):
+        for side in range(2):
+            j = quarter // 2 * 4 + side * 2 + quarter % 2
             for x in range(length):
-                work[y_half * (wide // 128) + j, x * pitch : x * pitch + orbs, :] = moved[
-                    x * orbs : (x + 1) * orbs, j * 128 : (j + 1) * 128
+                work[j, x * pitch : x * pitch + orbs, :] = moved[
+                    x * orbs : (x + 1) * orbs, side * 128 : (side + 1) * 128
                 ]
     for orb in range(orbs):
         for j in range(plane // 128):

time: 94 us -> 93.9 us (level)
  no operation moved by 1% of the time
where the time goes in v8:
time: 93.9 us; the launch traced here: 93.6 us
  blocking collectives  34.3 us (37%)
  waiting for transfers between devices  25.2 us (27%)
  Pallas kernels  19.3 us (21%)
  starting transfers between devices  11.2 us (12%)
  local copies, waits for them, and re-layouts  2.72 us (3%)
    all_to_all x1, blocking collectives, on_device(): lax.all_to_all(partial, 'orb', split_axis=0, concat_axis=0, tiled=True)  34.3 us
    all_to_all x1, waiting for transfers between devices, on_device(): lax.all_to_all(outgoing, 'orb', split_axis=0, concat_axis=0, tiled=True)  21.6 us
    pallas_call x1, Pallas kernels, call_solve(): pl.pallas_call(functools.partial(solve_kernel, orbs, pairs.shape[0] // 2)...  12.1 us
    all_to_all x1, starting transfers between devices, on_device(): lax.all_to_all(asking, 'orb', split_axis=0, concat_axis=0, tiled=True)  7.39 us
    all_to_all x1, starting transfers between devices, on_device(): lax.all_to_all(outgoing, 'orb', split_axis=0, concat_axis=0, tiled=True)  3.8 us
    pallas_call x1, Pallas kernels, on_device(): pl.pallas_call(final_kernel, grid=(2,), out_shape=jax.ShapeDtypeStruct((o...  3.64 us
    all_to_all x1, waiting for transfers between devices, on_device(): lax.all_to_all(asking, 'orb', split_axis=0, concat_axis=0, tiled=True)  3.63 us
    unnamed x18, local copies, waits for them, and re-layouts  2.39 us
  transfers between devices with their start and end apart: 2, of which 2 were waited for; matrix products, arithmetic and copies ran while one was open for 1% of the time, Pallas kernels for 1%

profile of v8, /device:TPU:0, one launch (start us, length us, event | category | flops | bytes accessed | tf_op | source)
XLA Modules:
  0.0 93.6 jit_solution(12087348947500839142)
XLA Ops:
  0.0 1.3 %ask.1 = s32[16,1,128]{2,1,0:T(1,128)} custom-call(s32[16]{0:T(128)} %bitcast.1), custom_call_target="tpu_custom_call" | custom-call | tf_op jit(solution)/shard_map/ask/pallas_call | solution.py:443
  1.3 7.4 %all-to-all-start = ((s32[16,1,128]{2,1,0:T(1,128)}), s32[16,1,128]{2,1,0:T(1,128)S(1)}, u32[]{:S(2)}, u32[]{:S(2)}) async-start(s32[16,1,128]{2,1,0:T(1,128)} %ask.1), calls=%async_computation | async-start | bytes 16384 | tf_op jit(solution)/shard_map/all_to_all | solution.py:459
  8.7 0.0 copy-start
  8.7 1.2 %copy-done = bf16[16,32768]{1,0:T(8,128)(2,1)S(1)} copy-done((bf16[16,32768]{1,0:T(8,128)(2,1)S(1)}, bf16[16,32768]{1,0:T(8,128)(2,1)}, u32[]{:S(2)}) %copy-start) | copy-done | bytes 1048600
  9.9 0.0 copy-start.4
  9.9 0.9 copy-done.4
  10.8 0.6 pack.1.packed_ref
  11.4 3.6 %all-to-all-done.asked_ref = s32[16,1,128]{2,1,0:T(1,128)S(1)} async-done(((s32[16,1,128]{2,1,0:T(1,128)}), s32[16,1,128]{2,1,0:T(1,128)S(1)}, u32[]{:S(2)}, u32[]{:S(2)}) %all-to-all-start) | async-done | bytes 8224 | tf_op jit(solution)/shard_map/all_to_all | solution.py:459
  15.0 1.8 %pick.1 = bf16[16,32,1024]{2,1,0:T(8,128)(2,1)} custom-call(s32[16,1,128]{2,1,0:T(1,128)S(1)} %all-to-all-done.asked_ref, bf16[16,32,1024]{2,1,0:T(8,128)(2,1)S(1)} %pack.1.packed_ref), custom_call_target="tpu_custom_call" | custom-call | tf_op jit(solution)/shard_map/pick/pallas_call | solution.py:460
  16.8 0.0 copy-start.7
  16.8 0.0 copy-start.5
  16.8 0.0 copy-start.6
  16.8 0.0 copy-start.1
  16.8 0.0 copy-start.2
  16.8 3.8 %all-to-all-start.1 = ((bf16[16,32,1024]{2,1,0:T(8,128)(2,1)}), bf16[16,32,1024]{2,1,0:T(8,128)(2,1)S(1)}, u32[]{:S(2)}, u32[]{:S(2)}) async-start(bf16[16,32,1024]{2,1,0:T(8,128)(2,1)} %pick.1), calls=%async_computation.1 | async-start | bytes 2097152 | tf_op jit(solution)/shard_map/all_to_all | solution.py:469
  21.3 0.0 copy-done.7
  21.3 0.1 copy.12
  21.4 0.1 reshape.11
  21.5 0.0 copy-done.5
  21.5 0.1 copy.11
  21.7 0.2 reshape.10
  21.9 0.0 copy-done.6
  21.9 0.1 pad_add_fusion.ints_ref
  22.0 21.6 %all-to-all-done.1.in_ref = bf16[16,32,1024]{2,1,0:T(8,128)(2,1)S(1)} async-done(((bf16[16,32,1024]{2,1,0:T(8,128)(2,1)}), bf16[16,32,1024]{2,1,0:T(8,128)(2,1)S(1)}, u32[]{:S(2)}, u32[]{:S(2)}) %all-to-all-start.1) | async-done | bytes 1048608 | tf_op jit(solution)/shard_map/all_to_all | solution.py:469
  43.5 0.0 copy-done.1
  43.5 0.0 copy-done.2
  43.5 12.1 %solve.1 = s16[16,272,128]{2,1,0:T(8,128)(2,1)S(1)} custom-call(s32[881]{0:T(1024)S(1)} %pad_add_fusion.ints_ref, bf16[16,32,1024]{2,1,0:T(8,128)(2,1)S(1)} %all-to-all-done.1.in_ref, bf16[352,768]{1,0:T(8,128)(2,1)S(1)} %copy-done.1, bf16[768,256]{1,0:T(8,128)(2,1)S(1)} %copy-done.2), custom_call_target="tpu_custom_call" | custom-call | tf_op jit(solution)/shard_map/solve/pallas_call | solution.py:409
  55.6 0.0 copy-start.3
  55.6 34.3 %all_to_all.15.in_ref.code_ref = s16[16,272,128]{2,1,0:T(8,128)(2,1)S(1)} all-to-all(s16[16,272,128]{2,1,0:T(8,128)(2,1)S(1)} %solve.1), channel_id=1, replica_groups=mesh['groups'=2,'orb'=16] {'orb'}, dimensions={0} | all-to-all | bytes 2228224 | tf_op jit(solution)/shard_map/all_to_all | solution.py:473
  90.0 0.0 copy-done.3
  90.0 3.6 %final.1 = f32[16,32768]{1,0:T(8,128)} custom-call(s32[16,1,128]{2,1,0:T(1,128)S(1)} %all-to-all-done.asked_ref, s16[16,272,128]{2,1,0:T(8,128)(2,1)S(1)} %all_to_all.15.in_ref.code_ref, s16[16,272,128]{2,1,0:T(8,128)(2,1)S(1)} %all_to_all.15.in_ref.code_ref, bf16[2,256,256]{2,1,0:T(8,128)(2,1)S(1)} %copy-done.3), custom_call_target="tpu_custom_call" | custom-call | tf_op jit(solution)/shard_map/final/pallas_call | solution.py:474
Async XLA Ops:
  1.3 13.7 %all-to-all-start = ((s32[16,1,128]{2,1,0:T(1,128)}), s32[16,1,128]{2,1,0:T(1,128)S(1)}, u32[]{:S(2)}, u32[]{:S(2)}) async-start(s32[16,1,128]{2,1,0:T(1,128)} %ask.1), calls=%async_computation | async-start | bytes 16384 | tf_op jit(solution)/shard_map/all_to_all | solution.py:459
  8.7 1.2 %copy-start = (bf16[16,32768]{1,0:T(8,128)(2,1)S(1)}, bf16[16,32768]{1,0:T(8,128)(2,1)}, u32[]{:S(2)}) copy-start(bf16[16,32768]{1,0:T(8,128)(2,1)} %phi_ref.1) | copy-start | bytes 3145732
  9.9 0.9 copy-start.4
  16.8 4.5 %copy-start.7 = (s32[48,2]{0,1:T(2,128)S(1)}, s32[48,2]{0,1:T(2,128)}, u32[]{:S(2)}) copy-start(s32[48,2]{0,1:T(2,128)} %param.12) | copy-start | bytes 1156
  16.8 4.7 %copy-start.5 = (s32[256,3]{0,1:T(4,128)S(1)}, s32[256,3]{0,1:T(4,128)}, u32[]{:S(2)}) copy-start(s32[256,3]{0,1:T(4,128)} %param.10) | copy-start | bytes 9220
  16.8 5.1 %copy-start.6 = (s32[1,16]{1,0:T(1,128)S(1)}, s32[1,16]{1,0:T(1,128)}, u32[]{:S(2)}) copy-start(s32[1,16]{1,0:T(1,128)} %param.11) | copy-start | bytes 196
  16.8 26.7 %copy-start.1 = (bf16[352,768]{1,0:T(8,128)(2,1)S(1)}, bf16[352,768]{1,0:T(8,128)(2,1)}, u32[]{:S(2)}) copy-start(bf16[352,768]{1,0:T(8,128)(2,1)} %constant.9.clone.var_ref) | copy-start | bytes 1622020
  16.8 26.7 %copy-start.2 = (bf16[768,256]{1,0:T(8,128)(2,1)S(1)}, bf16[768,256]{1,0:T(8,128)(2,1)}, u32[]{:S(2)}) copy-start(bf16[768,256]{1,0:T(8,128)(2,1)} %constant.10.clone.sine_hbm) | copy-start | bytes 1179652
  16.8 26.7 %all-to-all-start.1 = ((bf16[16,32,1024]{2,1,0:T(8,128)(2,1)}), bf16[16,32,1024]{2,1,0:T(8,128)(2,1)S(1)}, u32[]{:S(2)}, u32[]{:S(2)}) async-start(bf16[16,32,1024]{2,1,0:T(8,128)(2,1)} %pick.1), calls=%async_computation.1 | async-start | bytes 2097152 | tf_op jit(solution)/shard_map/all_to_all | solution.py:469
  55.6 34.4 %copy-start.3 = (bf16[2,256,256]{2,1,0:T(8,128)(2,1)S(1)}, bf16[2,256,256]{2,1,0:T(8,128)(2,1)}, u32[]{:S(2)}) copy-start(bf16[2,256,256]{2,1,0:T(8,128)(2,1)} %constant.11.clone.table_ref) | copy-start | bytes 786436
